TPU v7x, 256 devices: a whole 4x4x8 slice. The times are simulated.
256 devices in a mesh: order: 32 (over y, x, core), blk: 8 (over z).
Axes of the slice: x: 4, y: 4, z: 8, core: 2. Of those that a mesh axis runs over, the one named last changes fastest.
Arguments:
- right_side: float32 [2, 2, 256, 3072], P(None, None, 'order'), may hold values from -6 to 6
- start_guess: float32 [2, 2, 256, 3072], P(None, None, 'order'), may hold values from -6 to 6
- legendre: bfloat16 [256, 1536, 3072], P('order', 'blk'), may hold values from -0.15309311 to 0.15309311, as said below
- orders: int32 [256], P('order'), may hold values from 0 to 3071, as said below
- prior_inv: float32 [3072], replicated, may hold values from 0.1 to 10
- noise_inv: float32 [2, 1536, 6144], P(None, ('blk', 'order')), may hold values from 0.05 to 0.8
- pixel_flags: int32 [2, 1536, 6144], P(None, ('blk', 'order')), may hold values 0 or 1
Outputs:
- solution: float32 [2, 2, 256, 3072], P(None, None, 'order')
- residual: float32 [2, 2, 256, 3072], P(None, None, 'order')
Inputs may be any that keep to these rules, and one draw needn't show every extreme that they name: `orders`: distinct order numbers; 0 is among them, and entries 2k and 2k + 1 hold m and 3071 - m. `legendre`: zero wherever the degree is below the slot's order number.
All inputs are finite; a program needn't handle non-finite values. No bound on the sum of `pixel_flags` on one device may be relied on, other than what follows from the above.
Results may differ from a plain program's by a relative error of at most 0.0059.
Values may be sent and summed in bfloat16 or wider, within the bound.
A program may use at most 128 MiB of HBM per device.

v0:
```python
import jax
import jax.numpy as jnp
from jax import lax
from jax.sharding import PartitionSpec as P

ITERS = 2


def conjugate(right_side, start_guess, operator, inner_sum):
    solution = start_guess
    residual = right_side - operator(start_guess)
    direction = residual
    norm_now = inner_sum(residual, residual)
    for iteration in range(ITERS):
        image = operator(direction)
        step_size = (norm_now / inner_sum(direction, image))[:, None, None, None]
        solution = solution + step_size * direction
        residual = residual - step_size * image
        norm_next = inner_sum(residual, residual)
        direction = residual + (norm_next / norm_now)[:, None, None, None] * direction
        norm_now = norm_next
    return (solution, residual)


def per_device(right_side, start_guess, legendre, orders, prior_inv, noise_inv, pixel_flags):
    high = lax.Precision.HIGHEST
    all_orders = lax.all_gather(orders, "order", axis=0, tiled=True)
    pixels = noise_inv.shape[2]
    longitude = jnp.arange(pixels, dtype=jnp.int32)
    phase_index = all_orders[:, None] * longitude[None, :] % pixels
    angles = phase_index.astype(jnp.float32) * (2.0 * jnp.pi / pixels)
    weight = jnp.where(all_orders == 0, 1.0, 2.0).astype(jnp.float32) * pixels ** (-0.5)
    fourier_table = jnp.stack(
        [weight[:, None] * jnp.cos(angles), -weight[:, None] * jnp.sin(angles)]
    )
    degree_count = legendre.shape[2]
    degrees = jnp.arange(degree_count, dtype=jnp.int32)
    parity_sign = 1.0 - 2.0 * ((degrees[None, :] + orders[:, None]) % 2).astype(jnp.float32)
    parity_low = parity_sign.astype(jnp.bfloat16)
    pixel_weight = noise_inv * pixel_flags.astype(jnp.float32)

    def weighted_modes(cycle_modes):
        sky_map = jnp.einsum("rchkm,cmp->rhkp", cycle_modes, fourier_table, precision=high)
        analysed = jnp.einsum(
            "rhkp,cmp->rchkm", sky_map * pixel_weight[None], fourier_table, precision=high
        ).astype(jnp.bfloat16)
        return lax.all_to_all(analysed, "order", split_axis=4, concat_axis=3, tiled=True)

    def cycle_partial(rounded):
        hemispheres = jnp.stack([rounded, rounded * parity_low], axis=2)
        cycle_modes = jnp.einsum(
            "rchml,mjl->rchjm", hemispheres, legendre, preferred_element_type=jnp.float32
        )
        returned = weighted_modes(
            lax.all_to_all(cycle_modes, "order", split_axis=3, concat_axis=4, tiled=True)
        )
        partial_value = jnp.einsum(
            "rchjm,mjl->rchml", returned, legendre, preferred_element_type=jnp.float32
        )
        return partial_value[:, :, 0] + parity_sign * partial_value[:, :, 1]

    def operator(vector):
        summed = lax.psum(cycle_partial(vector.astype(jnp.bfloat16)), "blk")
        return prior_inv * vector + summed

    def inner_sum(first_vec, second_vec):
        return lax.psum(jnp.sum(first_vec * second_vec, axis=(1, 2, 3)), "order")

    solution, residual = conjugate(right_side, start_guess, operator, inner_sum)
    return (solution, residual)


def solution(mesh):
    in_specs = (
        P(None, None, "order", None),
        P(None, None, "order", None),
        P("order", "blk", None),
        P("order"),
        P(),
        P(None, ("blk", "order"), None),
        P(None, ("blk", "order"), None),
    )
    out_specs = (P(None, None, "order", None), P(None, None, "order", None))
    return jax.shard_map(
        per_device, mesh=mesh, in_specs=in_specs, out_specs=out_specs, check_vma=False
    )
```

profile of v0, /device:TPU:1, one launch (start us, length us, event | category | flops | bytes accessed | tf_op | source)
XLA Modules:
  0.0 679.2 jit_solution(776303709488587101)
XLA Ops:
  10.1 6.5 fusion.65
  18.9 8.6 %all-to-all-start = ((f32[32,1,384]{2,1,0:T(1,128)}), f32[32,1,384]{2,1,0:T(1,128)S(1)}, u32[]{:S(2)}, u32[]{:S(2)}) async-start(f32[32,1,384]{2,1,0:T(1,128)} %reshape.190), calls=%async_computation | async-start | bytes 98304 | tf_op jit(solution)/shard_map/all_to_all | solution.py:55
  29.1 13.5 %all-reduce = s32[256]{0:T(256)S(1)} all-reduce(s32[256]{0:T(256)S(1)} %dynamic-update-slice), channel_id=1, replica_groups=mesh['order'=32,'blk'=8] {'order'}, use_global_device_ids=true, to_apply=%add | all-reduce | flops 256 | bytes 2048
  42.6 28.3 %cosine_multiply_fusion = (f32[1,256,6144]{2,1,0:T(8,128)}, f32[1,256,6144]{2,1,0:T(8,128)}) fusion(s32[256]{0:T(256)S(1)} %all-reduce, f32[256]{0:T(256)S(1)} %get-tuple-element.30, f32[256]{0:T(256)S(1)} %get-tuple-element.31), kind=kLoop, calls=%fused_computation.38 | loop fusion | flops 17301504 | bytes 12585984 | tf_op jit(solution)/shard_map/mul | solution.py:34
  74.4 10.1 %fusion.48 = f32[2,2,6,6144,1]{3,2,1,0,4:T(8,128)S(1)} fusion(f32[1,256,6144]{2,1,0:T(8,128)} %get-tuple-element.29, f32[1,256,6144]{2,1,0:T(8,128)} %get-tuple-element.28, f32[2,6,6144]{2,1,0:T(8,128)S(1)} %copy.138, f32[2,2,2,6,256]{4,2,3,1,0:T(2,128)S(1)} %all_to_all.81), kind=kOutput, calls=%fused_computation.34 | convolution fusion | flops 909262848 | bytes 13516800 | tf_op jit(solution)/shard_map/rchkm,cmp->rhkp/dot_general | solution.py:43
  84.6 13.5 %fusion.89 = bf16[2,2,2,6,256]{4,3,2,0,1:T(8,128)(2,1)S(1)} fusion(f32[2,2,6,6144,1]{3,2,1,0,4:T(8,128)S(1)} %fusion.48, f32[1,256,6144]{2,1,0:T(8,128)} %get-tuple-element.29, f32[1,256,6144]{2,1,0:T(8,128)S(1)} %bitcast.232), kind=kOutput, calls=%fused_computation.54 | convolution fusion | flops 909127680 | bytes 13197312 | tf_op jit(solution)/shard_map/rhkp,cmp->rchkm/dot_general | solution.py:44
  99.9 13.8 %all_to_all.108 = bf16[32,2,192]{2,1,0:T(2,128)(2,1)S(1)} all-to-all(bf16[32,2,192]{2,1,0:T(2,128)(2,1)S(1)} %reshape.192), channel_id=1, replica_groups=mesh['order'=32,'blk'=8] {'order'}, dimensions={0} | all-to-all | bytes 49152 | tf_op jit(solution)/shard_map/all_to_all | solution.py:47
  123.1 67.5 %all-reduce.6.cloned.1.call-done = f32[2,2,8,3072]{3,1,0,2:T(2,128)} async-done(((f32[2,2,8,3072]{3,1,0,2:T(2,128)}), f32[2,2,8,3072]{3,1,0,2:T(2,128)}) %all-reduce.6.cloned.1.call-update) | async-done | bytes 393232 | tf_op jit(solution)/shard_map/psum | solution.py:63
  192.5 6.4 fusion.68
  200.6 19.4 %all_to_all.109 = f32[32,1,384]{2,1,0:T(1,128)S(1)} all-to-all(f32[32,1,384]{2,1,0:T(1,128)S(1)} %reshape.194), channel_id=1, replica_groups=mesh['order'=32,'blk'=8] {'order'}, dimensions={0} | all-to-all | bytes 98304 | tf_op jit(solution)/shard_map/all_to_all | solution.py:55
  224.8 10.1 %fusion.42 = f32[2,2,6,6144,1]{3,2,1,0,4:T(8,128)S(1)} fusion(f32[1,256,6144]{2,1,0:T(8,128)} %get-tuple-element.29, f32[1,256,6144]{2,1,0:T(8,128)} %get-tuple-element.28, f32[2,6,6144]{2,1,0:T(8,128)S(1)} %copy.138, f32[2,2,2,6,256]{4,2,3,1,0:T(2,128)S(1)} %all_to_all.89), kind=kOutput, calls=%fused_computation.32 | convolution fusion | flops 909262848 | bytes 13516800 | tf_op jit(solution)/shard_map/rchkm,cmp->rhkp/dot_general | solution.py:43
  235.0 13.5 %fusion.86 = bf16[2,2,2,6,256]{4,3,2,0,1:T(8,128)(2,1)S(1)} fusion(f32[2,2,6,6144,1]{3,2,1,0,4:T(8,128)S(1)} %fusion.42, f32[1,256,6144]{2,1,0:T(8,128)} %get-tuple-element.29, f32[1,256,6144]{2,1,0:T(8,128)S(1)} %bitcast.234), kind=kOutput, calls=%fused_computation.53 | convolution fusion | flops 909127680 | bytes 13197312 | tf_op jit(solution)/shard_map/rhkp,cmp->rchkm/dot_general | solution.py:44
  249.8 11.0 %all_to_all.110 = bf16[32,2,192]{2,1,0:T(2,128)(2,1)S(1)} all-to-all(bf16[32,2,192]{2,1,0:T(2,128)(2,1)S(1)} %reshape.196), channel_id=1, replica_groups=mesh['order'=32,'blk'=8] {'order'}, dimensions={0} | all-to-all | bytes 49152 | tf_op jit(solution)/shard_map/all_to_all | solution.py:47
  269.3 63.2 %all-reduce.8.cloned.1.call-done = f32[2,2,8,3072]{3,1,0,2:T(2,128)} async-done(((f32[2,2,8,3072]{3,1,0,2:T(2,128)}), f32[2,2,8,3072]{3,1,0,2:T(2,128)}) %all-reduce.8.cloned.1.call-update) | async-done | bytes 393232 | tf_op jit(solution)/shard_map/psum | solution.py:63
  334.1 67.2 %all-reduce.1 = (f32[2]{0:T(128)S(1)}, f32[2]{0:T(128)S(1)}) all-reduce(f32[2]{0:T(128)S(1)} %get-tuple-element.13, f32[2]{0:T(128)S(1)} %get-tuple-element.12), channel_id=1, replica_groups=mesh['order'=32,'blk'=8] {'order'}, use_global_device_ids=true, to_apply=%region_2.3 | all-reduce | flops 4 | bytes 32 | tf_op jit(solution)/shard_map/psum | solution.py:67
  402.8 62.7 %psum.53 = f32[2]{0:T(128)S(1)} all-reduce(f32[2]{0:T(128)S(1)} %get-tuple-element.18), channel_id=1, replica_groups=mesh['order'=32,'blk'=8] {'order'}, use_global_device_ids=true, to_apply=%region_7.8 | all-reduce | flops 2 | bytes 16 | tf_op jit(solution)/shard_map/psum | solution.py:67
  466.0 6.4 fusion.71
  474.2 11.0 %all_to_all.111 = f32[32,1,384]{2,1,0:T(1,128)S(1)} all-to-all(f32[32,1,384]{2,1,0:T(1,128)S(1)} %reshape.198), channel_id=1, replica_groups=mesh['order'=32,'blk'=8] {'order'}, dimensions={0} | all-to-all | bytes 98304 | tf_op jit(solution)/shard_map/all_to_all | solution.py:55
  492.0 10.1 %fusion.36 = f32[2,2,6,6144,1]{3,2,1,0,4:T(8,128)S(1)} fusion(f32[1,256,6144]{2,1,0:T(8,128)} %get-tuple-element.29, f32[1,256,6144]{2,1,0:T(8,128)} %get-tuple-element.28, f32[2,6,6144]{2,1,0:T(8,128)S(1)} %copy.138, f32[2,2,2,6,256]{4,2,3,1,0:T(2,128)S(1)} %all_to_all.97), kind=kOutput, calls=%fused_computation.30 | convolution fusion | flops 909262848 | bytes 13516800 | tf_op jit(solution)/shard_map/rchkm,cmp->rhkp/dot_general | solution.py:43
  502.1 13.5 %fusion.83 = bf16[2,2,2,6,256]{4,3,2,0,1:T(8,128)(2,1)S(1)} fusion(f32[2,2,6,6144,1]{3,2,1,0,4:T(8,128)S(1)} %fusion.36, f32[1,256,6144]{2,1,0:T(8,128)} %get-tuple-element.29, f32[1,256,6144]{2,1,0:T(8,128)S(1)} %bitcast.236), kind=kOutput, calls=%fused_computation.52 | convolution fusion | flops 909127680 | bytes 13197312 | tf_op jit(solution)/shard_map/rhkp,cmp->rchkm/dot_general | solution.py:44
  517.0 11.1 %all_to_all.112 = bf16[32,2,192]{2,1,0:T(2,128)(2,1)S(1)} all-to-all(bf16[32,2,192]{2,1,0:T(2,128)(2,1)S(1)} %reshape.200), channel_id=1, replica_groups=mesh['order'=32,'blk'=8] {'order'}, dimensions={0} | all-to-all | bytes 49152 | tf_op jit(solution)/shard_map/all_to_all | solution.py:47
  530.5 5.1 fusion.62
  536.6 63.2 %all-reduce.10.cloned.1.call-done = f32[2,2,8,3072]{3,1,0,2:T(2,128)} async-done(((f32[2,2,8,3072]{3,1,0,2:T(2,128)}), f32[2,2,8,3072]{3,1,0,2:T(2,128)}) %all-reduce.10.cloned.1.call-update) | async-done | bytes 393232 | tf_op jit(solution)/shard_map/psum | solution.py:63
  601.2 67.2 %psum.55 = f32[2]{0:T(128)S(1)} all-reduce(f32[2]{0:T(128)S(1)} %multiply_reduce_fusion), channel_id=1, replica_groups=mesh['order'=32,'blk'=8] {'order'}, use_global_device_ids=true, to_apply=%region_10.11 | all-reduce | flops 2 | bytes 16 | tf_op jit(solution)/shard_map/psum | solution.py:67
  (105 shorter events, 61.0 us)
Async XLA Ops:
  9.7 17.9 %copy-start.9 = (u32[256]{0:T(256)S(1)}, u32[256]{0:T(256)}, u32[]{:S(2)}) copy-start(u32[256]{0:T(256)} %constant.47) | copy-start | bytes 3076
  9.7 19.1 %copy-start.8 = (s32[8]{0:T(128)S(1)}, s32[8]{0:T(128)}, u32[]{:S(2)}) copy-start(s32[8]{0:T(128)} %param.10) | copy-start | bytes 100
  18.9 52.3 %all-to-all-start = ((f32[32,1,384]{2,1,0:T(1,128)}), f32[32,1,384]{2,1,0:T(1,128)S(1)}, u32[]{:S(2)}, u32[]{:S(2)}) async-start(f32[32,1,384]{2,1,0:T(1,128)} %reshape.190), calls=%async_computation | async-start | bytes 98304 | tf_op jit(solution)/shard_map/all_to_all | solution.py:55
  27.5 163.0 %all-reduce.6.cloned.1.call-start = ((), (), s32[]{:S(2)}) async-start(), calls=%async_computation.6 | async-start | bytes 786432 | tf_op jit(solution)/shard_map/psum | solution.py:63
  42.6 28.3 %copy-start.6 = (f32[2,6,6144]{2,0,1:T(2,128)S(1)}, f32[2,6,6144]{2,0,1:T(2,128)}, u32[]{:S(2)}) copy-start(f32[2,6,6144]{2,0,1:T(2,128)} %param.12) | copy-start | bytes 884740
  42.6 28.3 %copy-start.7 = (s32[2,6,6144]{2,0,1:T(2,128)S(1)}, s32[2,6,6144]{2,0,1:T(2,128)}, u32[]{:S(2)}) copy-start(s32[2,6,6144]{2,0,1:T(2,128)} %param.13) | copy-start | bytes 884740
  74.0 10.6 %slice-start = ((s8[6291456]{0:T(1024)(128)(4,1)}), s8[2097152]{0:T(1024)(128)(4,1)S(1)}, s32[]{:S(2)}) async-start(s8[6291456]{0:T(1024)(128)(4,1)} %bitcast.231), calls=%async_computation.9 | async-start | bytes 4194304
  74.4 10.2 %slice-start.1 = ((s8[6291456]{0:T(1024)(128)(4,1)}), s8[4194304]{0:T(1024)(128)(4,1)S(1)}, s32[]{:S(2)}) async-start(s8[6291456]{0:T(1024)(128)(4,1)} %bitcast.231), calls=%async_computation.10 | async-start | bytes 8388608
  116.0 74.5 %copy-start = (f32[2,2,8,3072]{3,2,1,0:T(8,128)S(1)}, f32[2,2,8,3072]{3,2,1,0:T(8,128)}, u32[]{:S(2)}) copy-start(f32[2,2,8,3072]{3,2,1,0:T(8,128)} %param.8) | copy-start | bytes 1179652
  116.1 74.5 %copy-start.4 = (f32[2,2,8,3072]{3,2,1,0:T(8,128)S(1)}, f32[2,2,8,3072]{3,2,1,0:T(8,128)}, u32[]{:S(2)}) copy-start(f32[2,2,8,3072]{3,2,1,0:T(8,128)} %param.7) | copy-start | bytes 1179652
  116.1 74.5 %copy-start.5 = (f32[3072]{0:T(1024)S(1)}, f32[3072]{0:T(1024)}, u32[]{:S(2)}) copy-start(f32[3072]{0:T(1024)} %param.11) | copy-start | bytes 36868
  123.0 209.4 %all-reduce.8.cloned.1.call-start = ((), (), s32[]{:S(2)}) async-start(), calls=%async_computation.7 | async-start | bytes 786432 | tf_op jit(solution)/shard_map/psum | solution.py:63
  223.1 11.8 %slice-start.2 = ((s8[6291456]{0:T(1024)(128)(4,1)}), s8[2097152]{0:T(1024)(128)(4,1)S(1)}, s32[]{:S(2)}) async-start(s8[6291456]{0:T(1024)(128)(4,1)} %bitcast.233), calls=%async_computation.11 | async-start | bytes 4194304
  224.8 10.1 %slice-start.3 = ((s8[6291456]{0:T(1024)(128)(4,1)}), s8[4194304]{0:T(1024)(128)(4,1)S(1)}, s32[]{:S(2)}) async-start(s8[6291456]{0:T(1024)(128)(4,1)} %bitcast.233), calls=%async_computation.12 | async-start | bytes 8388608
  269.2 330.6 %all-reduce.10.cloned.1.call-start = ((), (), s32[]{:S(2)}) async-start(), calls=%async_computation.8 | async-start | bytes 786432 | tf_op jit(solution)/shard_map/psum | solution.py:63
  402.8 70.2 %copy-start.2 = (f32[2,2,8,3072]{3,1,0,2:T(2,128)}, f32[2,2,8,3072]{3,1,0,2:T(2,128)S(1)}, u32[]{:S(2)}) copy-start(f32[2,2,8,3072]{3,1,0,2:T(2,128)S(1)} %get-tuple-element.19) | copy-start | bytes 1179652
  488.0 14.1 %slice-start.4 = ((s8[6291456]{0:T(1024)(128)(4,1)}), s8[2097152]{0:T(1024)(128)(4,1)S(1)}, s32[]{:S(2)}) async-start(s8[6291456]{0:T(1024)(128)(4,1)} %bitcast.235), calls=%async_computation.13 | async-start | bytes 4194304
  492.0 10.1 %slice-start.5 = ((s8[6291456]{0:T(1024)(128)(4,1)}), s8[4194304]{0:T(1024)(128)(4,1)S(1)}, s32[]{:S(2)}) async-start(s8[6291456]{0:T(1024)(128)(4,1)} %bitcast.235), calls=%async_computation.14 | async-start | bytes 8388608
  530.5 138.0 %copy-start.1 = (f32[2,2,8,3072]{3,2,1,0:T(8,128)S(1)}, f32[2,2,8,3072]{3,2,1,0:T(8,128)}, u32[]{:S(2)}) copy-start(f32[2,2,8,3072]{3,2,1,0:T(8,128)} %param.8) | copy-start | bytes 1179652
  530.5 138.0 %copy-start.3 = (f32[2,2,8,3072]{3,1,0,2:T(2,128)S(1)}, f32[2,2,8,3072]{3,1,0,2:T(2,128)}, u32[]{:S(2)}) copy-start(f32[2,2,8,3072]{3,1,0,2:T(2,128)} %copy-done.2) | copy-start | bytes 1179652
Sparse Core Ops, SparseCore 0:
  123.2 67.3 all-reduce.5
  269.4 63.0 all-reduce.7
  536.7 63.0 all-reduce.9
where the time goes:
time: 685 us; the launch traced here: 679 us
  blocking collectives  277 us (40%)
  waiting for transfers between devices  194 us (28%)
  matrix products  105 us (15%)
  other arithmetic  44.7 us (7%)
  local copies, waits for them, and re-layouts  34.3 us (5%)
  between operations  15.5 us (2%)
  starting transfers between devices  8.71 us (1%)
    psum x3, blocking collectives, inner_sum(): return lax.psum(jnp.sum(first_vec * second_vec, axis=(1, 2, 3)), 'order')  197 us
    psum x3, waiting for transfers between devices, operator(): summed = lax.psum(cycle_partial(vector.astype(jnp.bfloat16)), 'blk')  194 us
    dot_general x3, matrix products, weighted_modes(): jnp.einsum('rhkp,cmp->rchkm', sky_map * pixel_weight[None], fourier_table...  40.5 us
    all_to_all x3, blocking collectives, weighted_modes(): lax.all_to_all(analysed, 'order', split_axis=4, concat_axis=3, tiled=True)  36 us
    all_to_all x2, blocking collectives, cycle_partial(): lax.all_to_all(cycle_modes, 'order', split_axis=3, concat_axis=4, tiled=T...  30.3 us
    dot_general x3, matrix products, weighted_modes(): jnp.einsum('rchkm,cmp->rhkp', cycle_modes, fourier_table, precision=high)  30.3 us
    mul x1, other arithmetic, per_device(): weight[:, None] * jnp.cos(angles)  28.3 us
    dot_general x3, matrix products, cycle_partial(): jnp.einsum('rchml,mjl->rchjm', hemispheres, legendre, preferred_element_t...  19.2 us
  transfers between devices with their start and end apart: 4, of which 3 were waited for; matrix products, arithmetic and copies ran while one was open for 4% of the time, Pallas kernels for 0%

commit v1 on v0

v1 whole, which is shorter than its diff:
```python
import functools

import jax
import jax.numpy as jnp
from jax import lax
from jax.experimental import pallas as pl
from jax.experimental.pallas import tpu as pltpu
from jax.sharding import PartitionSpec as P

MESH = pl.DeviceIdType.MESH
F32 = jnp.float32
BF16 = jnp.bfloat16
VMEM_LIMIT = 56 * 1024 * 1024
NT = (((1,), (1,)), ((), ()))


def iota(shape, dim):
    return lax.broadcasted_iota(jnp.int32, shape, dim)


def pack_kernel(degrees, rows_step, orders, leg, rhs, guess, prior,
                leg_out, rhs_live, rhs_dead, x_live, x_dead, prior_live, prior_dead,
                mask_out, parity_out, row_a, row_b):
    pair = pl.program_id(0)
    block = pl.program_id(1)
    shift = orders[2 * pair]
    width = mask_out.shape[2]

    def rows_of(step, carry):
        rows = pl.ds(pl.multiple_of(step * 16, 16), 16)
        first = leg[0, 0, rows, :].astype(F32)
        second = pltpu.roll(leg[0, 1, rows, :].astype(F32), shift, 1)
        place = iota((16, degrees), 1)
        leg_out[0, rows, pl.ds(0, degrees)] = jnp.where(place >= shift, first, second).astype(BF16)
        extra = jnp.where(iota((16, 128), 1) == 0, second[:, degrees - 1:degrees], 0.0)
        leg_out[0, rows, pl.ds(degrees, 128)] = extra.astype(BF16)
        return carry

    lax.fori_loop(0, rows_step // 16, rows_of, 0)

    @pl.when((pair == 0) & (block == 0))
    def _():
        for quad in range(2):
            low, high = orders[4 * quad], orders[4 * quad + 2]
            low_b, high_b = orders[4 * quad + 1], orders[4 * quad + 3]
            upper = iota((8, degrees), 0) < 4
            shifts = jnp.where(upper, low, high)
            place = iota((8, degrees), 1)
            own = place >= shifts
            tail = iota((8, 128), 1) == 0

            def split(values_a, values_b, live, dead):
                rolled = jnp.where(upper, pltpu.roll(values_b, low, 1), pltpu.roll(values_b, high, 1))
                live[quad, :, pl.ds(0, degrees)] = jnp.where(own, values_a, rolled)
                live[quad, :, pl.ds(degrees, 128)] = jnp.where(tail, rolled[:, degrees - 1:degrees], 0.0)
                if width > degrees + 128:
                    live[quad, :, pl.ds(degrees + 128, width - degrees - 128)] = jnp.zeros(
                        (8, width - degrees - 128), F32)
                dead_values = jnp.where(own, rolled, values_a)
                dead[quad] = jnp.where(place == degrees - 1, 0.0, dead_values)

            for source, live, dead in ((rhs, rhs_live, rhs_dead), (guess, x_live, x_dead)):
                for half in range(2):
                    slot = 4 * quad + 2 * half
                    for r in range(2):
                        for c in range(2):
                            at = half * 4 + r * 2 + c
                            row_a[at:at + 1, :] = source[r, c, slot:slot + 1, :]
                            row_b[at:at + 1, :] = source[r, c, slot + 1:slot + 2, :]
                split(row_a[...], row_b[...], live, dead)
            every = jnp.broadcast_to(prior[...], (8, degrees))
            split(every, every, prior_live, prior_dead)
            degree = jnp.where(own, place, place - shifts + degrees)
            number = jnp.where(own, shifts, jnp.where(upper, low_b, high_b))
            parity = 1 - 2 * ((degree + number) & 1)
            parity_out[quad, :, pl.ds(0, degrees)] = parity.astype(F32)
            parity_out[quad, :, pl.ds(degrees, width - degrees)] = jnp.ones((8, width - degrees), F32)
            mask_out[quad, :, pl.ds(0, degrees)] = own.astype(F32)
            mask_out[quad, :, pl.ds(degrees, width - degrees)] = jnp.zeros((8, width - degrees), F32)


def unpack_kernel(degrees, orders, x_live, x_dead, r_live, r_dead, x_out, r_out, row_b):
    for quad in range(2):
        low, high = orders[4 * quad], orders[4 * quad + 2]
        upper = iota((8, degrees), 0) < 4
        place = iota((8, degrees), 1)
        own = place >= jnp.where(upper, low, high)
        for live, dead, out in ((x_live, x_dead, x_out), (r_live, r_dead, r_out)):
            alive = live[quad, :, pl.ds(0, degrees)]
            idle = dead[quad]
            values_a = jnp.where(own, alive, idle)
            values_b = jnp.where(own, idle, alive)
            extra = live[quad, :, pl.ds(degrees, 128)][:, 0:1]
            values_b = jnp.where(place == degrees - 1, extra, values_b)
            back = jnp.where(upper,
                             pltpu.roll(values_b, lax.rem(degrees - low, degrees), 1),
                             pltpu.roll(values_b, lax.rem(degrees - high, degrees), 1))
            row_b[0] = values_a
            row_b[1] = back
            for half in range(2):
                slot = 4 * quad + 2 * half
                for r in range(2):
                    for c in range(2):
                        at = half * 4 + r * 2 + c
                        out[r, c, slot:slot + 1, :] = row_b[0, at:at + 1, :]
                        out[r, c, slot + 1:slot + 2, :] = row_b[1, at:at + 1, :]


def split_bf16(values):
    high = values.astype(BF16)
    return high, (values - high.astype(F32)).astype(BF16)


def main_kernel(n_order, n_blk, degrees, cycles, pixels,
                own_orders, leg, rhs_live, rhs_dead, x_live, x_dead, prior_live, prior_dead,
                mask, parity, noise, flags,
                x_out_live, x_out_dead, r_out_live, r_out_dead,
                live, dead, lhs, modes, turned, back, send, recv, order_recv, scalar,
                flhs, weight, anal, sign, current, turn, table_hi, table_lo,
                partial, shard, rs_recv, summed, r1_live, r1_dead, steps,
                order_sems, a2a_send, a2a_recv, rs_send, rs_recv_sem, ag_send, ag_recv):
    me = lax.axis_index("order")
    mine = lax.axis_index("blk")
    width = degrees + 128
    half_turn = pixels // 2
    columns = 16 * n_order
    groups = columns // 128
    local = cycles * n_order
    shard_lanes = shard.shape[1]
    per_quad = n_blk // 2
    sheets = modes.shape[0]

    barrier = pltpu.get_barrier_semaphore()

    def greet_order(i, carry):
        pl.semaphore_signal(barrier, inc=1, device_id=(lax.rem(me + i, n_order), mine), device_id_type=MESH)
        return carry

    def greet_blk(i, carry):
        pl.semaphore_signal(barrier, inc=1, device_id=(me, lax.rem(mine + i, n_blk)), device_id_type=MESH)
        return carry

    lax.fori_loop(1, n_order, greet_order, 0)
    lax.fori_loop(1, n_blk, greet_blk, 0)

    weight[...] = jnp.zeros_like(weight)
    for h in range(2):
        for image in range(2):
            at = pl.ds(image * half_turn, half_turn)
            value = noise[h, :, at] * flags[h, :, at].astype(F32)
            for r in range(2):
                weight[image * 4 + h * 2 + r, 0:cycles, :] = value
    modes[...] = jnp.zeros_like(modes)
    turned[...] = jnp.zeros_like(turned)
    partial[...] = jnp.zeros_like(partial)
    scalar[...] = jnp.zeros_like(scalar)
    live[0] = x_live[...]
    dead[0] = x_dead[...]

    pl.semaphore_wait(barrier, n_order - 1 + n_blk - 1)

    def order_copy(i):
        return pltpu.make_async_remote_copy(
            src_ref=own_orders, dst_ref=order_recv.at[me],
            send_sem=order_sems.at[0], recv_sem=order_sems.at[1],
            device_id=(lax.rem(me + i, n_order), mine), device_id_type=MESH)

    def order_start(i, carry):
        order_copy(i).start()
        return carry

    lax.fori_loop(1, n_order, order_start, 0)
    order_recv[me] = own_orders[...]

    def wait_bytes(ref, sem):
        pltpu.make_async_copy(ref, ref, sem).wait()

    def exchange_start(step):
        def one(i, carry):
            to = lax.rem(me + i, n_order)
            pltpu.make_async_remote_copy(
                src_ref=send.at[to], dst_ref=recv.at[step, me],
                send_sem=a2a_send.at[step], recv_sem=a2a_recv.at[step],
                device_id=(to, mine), device_id_type=MESH).start()
            return carry

        lax.fori_loop(1, n_order, one, 0)

    def exchange_wait(step):
        wait_bytes(recv.at[step, pl.ds(0, n_order - 1)], a2a_recv.at[step])
        wait_bytes(send.at[pl.ds(0, n_order - 1)], a2a_send.at[step])
        recv[step, me] = send[me]

    def build_table():
        wait_bytes(order_recv.at[pl.ds(0, n_order - 1)], order_sems.at[1])
        wait_bytes(order_recv.at[pl.ds(0, n_order - 1)], order_sems.at[0])
        number = order_recv[...]
        lane = iota((n_order, 8, 128), 2)
        number_f = number.astype(F32)
        scale = jnp.where(number == 0, 1.0, 2.0) * (pixels ** -0.5)

        def angle(product):
            value = product.astype(F32)
            value = value - pixels * jnp.floor(value * (1.0 / pixels))
            return value * (2.0 * jnp.pi / pixels)

        base = angle(number * lane)
        current[:, 0] = scale * jnp.cos(base)
        current[:, 1] = -scale * jnp.sin(base)
        step = angle(number * 128)
        turn[:, 0] = jnp.cos(step)
        turn[:, 1] = jnp.sin(step)
        odd = (1 - 2 * (number & 1)).astype(F32)
        sign_rows = jnp.concatenate([odd, odd], axis=1).reshape(columns, 128)
        sign[...] = sign_rows.T[0:8]

        def block(q, carry):
            lanes = pl.ds(pl.multiple_of(q * 128, 128), 128)

            def some(part, inner):
                for k in range(8):
                    s = part * 8 + k
                    cosine, sine = current[s, 0], current[s, 1]
                    rows = pl.ds(pl.multiple_of(s * 16, 16), 16)
                    both = jnp.concatenate([cosine, sine], axis=0)
                    high, rest = split_bf16(both)
                    table_hi[rows, lanes] = high
                    table_lo[rows, lanes] = rest
                    turn_c, turn_s = turn[s, 0], turn[s, 1]
                    current[s, 0] = cosine * turn_c + sine * turn_s
                    current[s, 1] = sine * turn_c - cosine * turn_s
                return inner

            return lax.fori_loop(0, n_order // 8, some, carry)

        lax.fori_loop(0, half_turn // 128, block, 0)

    row8 = iota((8, 128), 0)
    lane8 = iota((8, 128), 1)
    group8 = lane8 // 16
    spare = lane8 >= 64

    def inner(first_live, second_live, first_dead, second_dead):
        total = jnp.zeros((8, 1), F32)
        for quad in range(2):
            total = total + jnp.sum(first_live(quad) * second_live(quad), axis=1, keepdims=True)
            total = total + jnp.sum(first_dead(quad) * second_dead(quad), axis=1, keepdims=True)
        first_row = (iota((8, 1), 0) % 4) < 2
        zero = jnp.sum(jnp.where(first_row, total, 0.0), axis=0, keepdims=True)
        one = jnp.sum(jnp.where(first_row, 0.0, total), axis=0, keepdims=True)
        return zero, one

    def put_scalars(values):
        tile = jnp.zeros((8, 128), F32)
        for at, value in enumerate(values):
            tile = jnp.where(row8 == at, value, tile)
        return jnp.where(spare, tile, 0.0)

    def sum_of(step):
        total = recv[step, 0]
        for s in range(1, n_order):
            total = total + recv[step, s]
        return total

    def by_row(total, at):
        return jnp.where((iota((8, 1), 0) % 4) < 2, total[at:at + 1, 64:65], total[at + 1:at + 2, 64:65])

    lane_step = 128 * max(n for n in (5, 3, 1) if (width // 128) % n == 0)

    def application(p, carry):
        for quad in range(2):
            def build(t, inner_carry):
                at = pl.ds(pl.multiple_of(t * lane_step, 128), lane_step)
                value = live[p, quad, :, at]
                first = mask[quad, :, at]
                second = 1.0 - first
                flip = parity[quad, :, at]
                high = value.astype(BF16).astype(F32)
                rest = value - high
                pieces = []
                for part in (high, rest):
                    for keep in (first, second):
                        kept = part * keep
                        pieces.append(kept)
                        pieces.append(kept * flip)
                lhs[quad, :, at] = jnp.concatenate(pieces, axis=0).astype(BF16)
                return inner_carry

            lax.fori_loop(0, width // lane_step, build, 0)
        for pair in range(4):
            quad, half = pair // 2, pair % 2
            out = lax.dot_general(lhs[quad], leg[pair], NT, preferred_element_type=F32)
            out = out[0:32] + out[32:64]
            at = 4 * half
            for slot in range(2):
                rows = jnp.concatenate([out[16 * slot + at:16 * slot + at + 4],
                                        out[16 * slot + 8 + at:16 * slot + 8 + at + 4]], axis=0)
                if sheets * 128 > local:
                    rows = jnp.concatenate([rows, jnp.zeros((8, sheets * 128 - local), F32)], axis=1)
                for sheet in range(sheets):
                    modes[sheet, pl.ds(2 * pair + slot, 8, stride=8), :] = rows[:, 128 * sheet:128 * sheet + 128]
        for sheet in range(sheets):
            turned[128 * sheet:128 * sheet + 128, :] = modes[sheet].T

        @pl.when(p == 2)
        def _():
            norm = inner(lambda q: live[1, q], lambda q: live[1, q], lambda q: dead[1, q], lambda q: dead[1, q])
            cross = inner(lambda q: live[1, q], lambda q: live[2, q], lambda q: dead[1, q], lambda q: dead[2, q])
            scalar[...] = put_scalars(norm + cross)

        for d in range(n_order):
            send[d] = turned[cycles * d:cycles * d + 8, :] + scalar[...]
        exchange_start(2 * p)

        @pl.when(p == 0)
        def _():
            build_table()

        exchange_wait(2 * p)

        @pl.when(p == 2)
        def _():
            total = sum_of(2 * p)
            norm, cross = by_row(total, 0), by_row(total, 2)
            step = norm / cross
            steps[0] = jnp.broadcast_to(norm, (8, 128))
            steps[1] = jnp.broadcast_to(step, (8, 128))
            for quad in range(2):
                r1_live[quad] = live[1, quad] - step * live[2, quad]
                r1_dead[quad] = dead[1, quad] - step * dead[2, quad]
            after = inner(lambda q: r1_live[q], lambda q: r1_live[q], lambda q: r1_dead[q], lambda q: r1_dead[q])
            scalar[...] = put_scalars(after)

        def shuffle(g, inner_carry):
            lanes = pl.ds(pl.multiple_of(g * 128, 128), 128)
            flip = sign[:, lanes]
            tiles = [recv[2 * p, g * 8 + i] for i in range(8)]
            straight = []
            for hr in range(4):
                acc = tiles[0] if hr == 0 else pltpu.roll(tiles[0], (128 - 16 * hr) % 128, 1)
                for i in range(1, 8):
                    by = (16 * i - 16 * hr) % 128
                    moved = tiles[i] if by == 0 else pltpu.roll(tiles[i], by, 1)
                    acc = jnp.where(group8 == i, moved, acc)
                straight.append(acc)
            flipped = [acc * flip for acc in straight]
            rows = jnp.concatenate(straight + flipped, axis=0)
            high, rest = split_bf16(rows)
            flhs[0:64, lanes] = high
            flhs[64:128, lanes] = rest
            return inner_carry

        lax.fori_loop(0, groups, shuffle, 0)

        anal[...] = jnp.zeros_like(anal)
        chunk = min(512, half_turn)

        def fourier(t, inner_carry):
            lanes = pl.ds(pl.multiple_of(t * chunk, 128), chunk)
            high_t, low_t = table_hi[:, lanes], table_lo[:, lanes]
            sky = jnp.dot(flhs[...], high_t, preferred_element_type=F32)
            sky = sky[0:64] + sky[64:128] + jnp.dot(flhs[0:64, :], low_t, preferred_element_type=F32)
            value = sky * weight[:, :, lanes].reshape(64, chunk)
            high, rest = split_bf16(value)
            out = lax.dot_general(jnp.concatenate([high, rest], axis=0), high_t, NT, preferred_element_type=F32)
            anal[...] += out[0:64] + out[64:128] + lax.dot_general(high, low_t, NT, preferred_element_type=F32)
            return inner_carry

        lax.fori_loop(0, half_turn // chunk, fourier, 0)

        def shuffle_back(g, inner_carry):
            lanes = pl.ds(pl.multiple_of(g * 128, 128), 128)
            flip = sign[:, lanes]
            rows = [anal[8 * hr:8 * hr + 8, lanes] + flip * anal[32 + 8 * hr:40 + 8 * hr, lanes] for hr in range(4)]
            base = scalar[...]
            for i in range(8):
                acc = base
                for hr in range(4):
                    by = (16 * hr - 16 * i) % 128
                    moved = rows[hr] if by == 0 else pltpu.roll(rows[hr], by, 1)
                    acc = jnp.where(group8 == hr, moved, acc)
                send[g * 8 + i] = acc
            return inner_carry

        lax.fori_loop(0, groups, shuffle_back, 0)
        exchange_start(2 * p + 1)
        exchange_wait(2 * p + 1)

        for d in range(n_order):
            turned[cycles * d:cycles * d + cycles, :] = recv[2 * p + 1, d, 0:cycles, :]
        for sheet in range(sheets):
            back[sheet] = turned[128 * sheet:128 * sheet + 128, :].T

        def rs_copy(b):
            return pltpu.make_async_remote_copy(
                src_ref=partial.at[b // per_quad, :, pl.ds((b % per_quad) * shard_lanes, shard_lanes)],
                dst_ref=rs_recv.at[p, mine],
                send_sem=rs_send.at[p], recv_sem=rs_recv_sem.at[p],
                device_id=(me, b), device_id_type=MESH)

        for quad in range(2):
            for half in range(2):
                pair = 2 * quad + half
                rows = jnp.concatenate([
                    jnp.concatenate([back[sheet, pl.ds(2 * pair + slot, 8, stride=8), :] for sheet in range(sheets)],
                                    axis=1)
                    for slot in range(2)], axis=0)
                high, rest = split_bf16(rows[:, 0:local])
                both = jnp.concatenate([high, rest], axis=0)

                def analyse(t, inner_carry):
                    at = pl.ds(pl.multiple_of(t * lane_step, 128), lane_step)
                    out = jnp.dot(both, leg[pair, :, at], preferred_element_type=F32)
                    out = out[0:16] + out[16:32]
                    first = mask[quad, 4 * half:4 * half + 1, at]
                    flip = parity[quad, 4 * half:4 * half + 1, at]
                    kept = jnp.where(first > 0.5, out[0:8], out[8:16])
                    partial[quad, 4 * half:4 * half + 4, at] = kept[0:4] + flip * kept[4:8]
                    return inner_carry

                lax.fori_loop(0, width // lane_step, analyse, 0)
            for b in range(per_quad * quad, per_quad * quad + per_quad):
                @pl.when(mine != b)
                def _():
                    rs_copy(b).start()

        wait_bytes(rs_recv.at[p, pl.ds(0, n_blk - 1)], rs_recv_sem.at[p])
        wait_bytes(rs_recv.at[p, pl.ds(0, n_blk - 1)], rs_send.at[p])
        my_quad = mine // per_quad
        my_lanes = pl.ds(pl.multiple_of((mine % per_quad) * shard_lanes, 128), shard_lanes)
        rs_recv[p, mine] = partial[my_quad, :, my_lanes]
        total = rs_recv[p, 0]
        for b in range(1, n_blk):
            total = total + rs_recv[p, b]
        shard[...] = total

        def ag_start(i, inner_carry):
            pltpu.make_async_remote_copy(
                src_ref=shard, dst_ref=summed.at[p, my_quad, :, my_lanes],
                send_sem=ag_send.at[p], recv_sem=ag_recv.at[p],
                device_id=(me, lax.rem(mine + i, n_blk)), device_id_type=MESH).start()
            return inner_carry

        lax.fori_loop(1, n_blk, ag_start, 0)
        summed[p, my_quad, :, my_lanes] = total
        wait_bytes(rs_recv.at[p, pl.ds(0, n_blk - 1)], ag_recv.at[p])
        wait_bytes(rs_recv.at[p, pl.ds(0, n_blk - 1)], ag_send.at[p])

        for quad in range(2):
            image = prior_live[quad] * live[p, quad] + summed[p, quad]
            live[p + 1, quad] = jnp.where(p == 0, rhs_live[quad] - image, image)
            image = prior_dead[quad] * dead[p, quad]
            dead[p + 1, quad] = jnp.where(p == 0, rhs_dead[quad] - image, image)
        return carry

    lax.fori_loop(0, 3, application, 0)

    after = by_row(sum_of(5), 0)
    ratio = after / steps[0, :, 0:1]
    step = steps[1, :, 0:1]

    def direction(q, r1, stored):
        return r1[q] + ratio * stored[1, q]

    def image_of(q, stored):
        return (1.0 + ratio) * stored[2, q] - step * stored[3, q]

    curve = inner(lambda q: direction(q, r1_live, live), lambda q: image_of(q, live),
                  lambda q: direction(q, r1_dead, dead), lambda q: image_of(q, dead))
    tile = put_scalars(curve)
    for d in range(n_order):
        send[d] = tile
    exchange_start(6)
    exchange_wait(6)
    second = after / by_row(sum_of(6), 0)
    for q in range(2):
        for r1, stored, x_out, r_out in ((r1_live, live, x_out_live, r_out_live),
                                         (r1_dead, dead, x_out_dead, r_out_dead)):
            x_out[q] = stored[0, q] + step * stored[1, q] + second * direction(q, r1, stored)
            r_out[q] = r1[q] - second * image_of(q, stored)


def per_device(n_order, n_blk, right_side, start_guess, legendre, orders, prior_inv, noise_inv, pixel_flags):
    slots, local, degrees = legendre.shape
    cycles, pixels = noise_inv.shape[1], noise_inv.shape[2]
    unit = 128 * (n_blk // 2)
    width = -(-(degrees + 128) // unit) * unit
    shard_lanes = width // (n_blk // 2)
    rows_step = local // 2 if (local // 2) % 16 == 0 else local
    smem = pl.BlockSpec(memory_space=pltpu.SMEM)
    vmem = pl.BlockSpec(memory_space=pltpu.VMEM)
    live_shape = jax.ShapeDtypeStruct((2, 8, width), F32)
    dead_shape = jax.ShapeDtypeStruct((2, 8, degrees), F32)

    packed = pl.pallas_call(
        functools.partial(pack_kernel, degrees, rows_step),
        grid=(4, local // rows_step),
        in_specs=[smem, pl.BlockSpec((1, 2, rows_step, degrees), lambda k, b: (k, 0, b, 0)), vmem, vmem, vmem],
        out_specs=[pl.BlockSpec((1, rows_step, degrees + 128), lambda k, b: (k, b, 0))] + [vmem] * 8,
        out_shape=[jax.ShapeDtypeStruct((4, local, degrees + 128), BF16),
                   live_shape, dead_shape, live_shape, dead_shape, live_shape, dead_shape, live_shape, live_shape],
        scratch_shapes=[pltpu.VMEM((8, degrees), F32), pltpu.VMEM((8, degrees), F32)],
        compiler_params=pltpu.CompilerParams(vmem_limit_bytes=VMEM_LIMIT),
        name="pack",
    )(orders, legendre.reshape(4, 2, local, degrees), right_side, start_guess, prior_inv.reshape(1, degrees))
    leg, rhs_live, rhs_dead, x_live, x_dead, prior_live, prior_dead, mask, parity = packed

    columns = 16 * n_order
    turned_rows = -(-(local + 8) // 128) * 128
    half_turn = pixels // 2
    own_orders = jnp.broadcast_to(orders[:, None], (8, 128))
    scratch = [
        pltpu.VMEM((4, 2, 8, width), F32),
        pltpu.VMEM((4, 2, 8, degrees), F32),
        pltpu.VMEM((2, 64, degrees + 128), BF16),
        pltpu.VMEM((turned_rows // 128, 128, 128), F32),
        pltpu.VMEM((turned_rows, 128), F32),
        pltpu.VMEM((turned_rows // 128, 128, 128), F32),
        pltpu.VMEM((n_order, 8, 128), F32),
        pltpu.VMEM((7, n_order, 8, 128), F32),
        pltpu.VMEM((n_order, 8, 128), jnp.int32),
        pltpu.VMEM((8, 128), F32),
        pltpu.VMEM((128, columns), BF16),
        pltpu.VMEM((8, 8, half_turn), F32),
        pltpu.VMEM((64, columns), F32),
        pltpu.VMEM((8, columns), F32),
        pltpu.VMEM((n_order, 2, 8, 128), F32),
        pltpu.VMEM((n_order, 2, 8, 128), F32),
        pltpu.VMEM((columns, half_turn), BF16),
        pltpu.VMEM((columns, half_turn), BF16),
        pltpu.VMEM((2, 8, width), F32),
        pltpu.VMEM((8, shard_lanes), F32),
        pltpu.VMEM((3, n_blk, 8, shard_lanes), F32),
        pltpu.VMEM((3, 2, 8, width), F32),
        pltpu.VMEM((2, 8, width), F32),
        pltpu.VMEM((2, 8, degrees), F32),
        pltpu.VMEM((2, 8, 128), F32),
        pltpu.SemaphoreType.DMA((2,)),
        pltpu.SemaphoreType.DMA((7,)),
        pltpu.SemaphoreType.DMA((7,)),
        pltpu.SemaphoreType.DMA((3,)),
        pltpu.SemaphoreType.DMA((3,)),
        pltpu.SemaphoreType.DMA((3,)),
        pltpu.SemaphoreType.DMA((3,)),
    ]
    results = pl.pallas_call(
        functools.partial(main_kernel, n_order, n_blk, degrees, cycles, pixels),
        in_specs=[vmem] * 12,
        out_specs=[vmem] * 4,
        out_shape=[live_shape, dead_shape, live_shape, dead_shape],
        scratch_shapes=scratch,
        compiler_params=pltpu.CompilerParams(
            collective_id=0, has_side_effects=True, vmem_limit_bytes=VMEM_LIMIT),
        name="steps",
    )(own_orders, leg, rhs_live, rhs_dead, x_live, x_dead, prior_live, prior_dead, mask, parity,
      noise_inv, pixel_flags)

    full = jax.ShapeDtypeStruct(right_side.shape, F32)
    return tuple(pl.pallas_call(
        functools.partial(unpack_kernel, degrees),
        in_specs=[smem] + [vmem] * 4,
        out_specs=[vmem] * 2,
        out_shape=[full, full],
        scratch_shapes=[pltpu.VMEM((2, 8, degrees), F32)],
        compiler_params=pltpu.CompilerParams(vmem_limit_bytes=VMEM_LIMIT),
        name="unpack",
    )(orders, *results))


def solution(mesh):
    in_specs = (
        P(None, None, "order", None),
        P(None, None, "order", None),
        P("order", "blk", None),
        P("order"),
        P(),
        P(None, ("blk", "order"), None),
        P(None, ("blk", "order"), None),
    )
    out_specs = (P(None, None, "order", None), P(None, None, "order", None))
    body = functools.partial(per_device, mesh.shape["order"], mesh.shape["blk"])
    return jax.shard_map(body, mesh=mesh, in_specs=in_specs, out_specs=out_specs, check_vma=False)
```

time: 685 us -> 157 us (0.23)
  blocking collectives: 277 us -> 0 us
  waiting for transfers between devices: 194 us -> 0 us
  Pallas kernels: 0 us -> 151 us
  matrix products: 105 us -> 0 us
  other arithmetic: 44.7 us -> 0 us
  local copies, waits for them, and re-layouts: 34.3 us -> 5.09 us
  between operations: 15.5 us -> 0.64 us
  starting transfers between devices: 8.71 us -> 0 us
    psum x3 -> x0, blocking collectives: 197 us -> none  [inner_sum(): return lax.psum(jnp.sum(first_vec * second_vec, axis=(1, 2, 3)), 'order')]
    psum x3 -> x0, waiting for transfers between devices: 194 us -> none  [operator(): summed = lax.psum(cycle_partial(vector.astype(jnp.bfloat16)), 'blk')]
    pallas_call x0 -> x3, Pallas kernels: none -> 151 us  [the longest x1 132 us: per_device(): pl.pallas_call(functools.partial(main_kernel, n_order, n_blk, degrees, cy...]
    dot_general x12 -> x0, matrix products: 105 us -> none  [the longest x3 40.5 us: weighted_modes(): jnp.einsum('rhkp,cmp->rchkm', sky_map * pixel_weight[None], fourier_table...]
    all_to_all x5 -> x0, blocking collectives: 66.3 us -> none  [the longest x3 36 us: weighted_modes(): lax.all_to_all(analysed, 'order', split_axis=4, concat_axis=3, tiled=True)]
    mul x3 -> x0, other arithmetic: 28.4 us -> none  [the longest x1 28.3 us: per_device(): weight[:, None] * jnp.cos(angles)]
    unnamed x49 -> x2, local copies, waits for them, and re-layouts: 17.8 us -> 3.77 us
    unnamed x1 -> x0, blocking collectives: 13.5 us -> none
  transfers between devices with their start and end apart: 4 -> 0, of which waited for: 3 -> 0; matrix products, arithmetic and copies ran while one was open for 4% -> 0% of each run, Pallas kernels for 0% -> 0%
where the time goes in v1:
time: 157 us; the launch traced here: 156 us
  Pallas kernels  151 us (96%)
  local copies, waits for them, and re-layouts  5.09 us (3%)
    pallas_call x1, Pallas kernels, per_device(): pl.pallas_call(functools.partial(main_kernel, n_order, n_blk, degrees, cy...  132 us
    pallas_call x1, Pallas kernels, per_device(): pl.pallas_call(functools.partial(pack_kernel, degrees, rows_step), grid=(...  15.5 us
    unnamed x2, local copies, waits for them, and re-layouts  3.77 us

profile of v1, /device:TPU:1, one launch (start us, length us, event | category | flops | bytes accessed | tf_op | source)
XLA Modules:
  0.0 156.3 jit_solution(5525994079573698444)
XLA Ops:
  0.6 1.3 broadcast_in_dim.2.own_orders
  1.9 1.9 %copy.9.noise = f32[2,6,6144]{2,1,0:T(8,128)} copy(f32[2,6,6144]{2,0,1:T(2,128)} %param.12) | data formatting | bytes 589824 | tf_op args[5]
  3.8 1.9 %copy.10.flags = s32[2,6,6144]{2,1,0:T(8,128)} copy(s32[2,6,6144]{2,0,1:T(2,128)} %param.13) | data formatting | bytes 589824 | tf_op args[6]
  5.7 15.5 %pack.1 = (bf16[4,192,3200]{2,1,0:T(8,128)(2,1)}, f32[2,8,3584]{2,1,0:T(8,128)}, f32[2,8,3072]{2,1,0:T(8,128)}, f32[2,8,3584]{2,1,0:T(8,128)}, f32[2,8,3072]{2,1...) custom-call(s32[8]{0:T(128)} %orders.3, ...), custom_call_target="tpu_custom_call" | custom-call | tf_op jit(solution)/shard_map/pack/pallas_call | solution.py:495
  21.2 132.3 %steps.1 = (f32[2,8,3584]{2,1,0:T(8,128)}, f32[2,8,3072]{2,1,0:T(8,128)}, f32[2,8,3584]{2,1,0:T(8,128)}, f32[2,8,3072]{2,1,0:T(8,128)}) custom-call(s32[8,128]{1,0:T(8,128)} %broadcast_in_dim.2.own_orders, bf16[4,192,3200]{2,1,0:T(8,128)(2,1)} %get-tuple-element.15.leg, f32[2,8,3584]{2,1,0:T(8,128)} %get-tuple-element.16.rhs_live, ...), custom_call_target="tpu_custom_call" | custom-call | tf_op jit(solution)/shard_map/steps/pallas_call | solution.py:546
  153.5 2.7 %unpack.1 = (f32[2,2,8,3072]{3,2,1,0:T(8,128)}, f32[2,2,8,3072]{3,2,1,0:T(8,128)}) custom-call(s32[8]{0:T(128)} %orders.3, f32[2,8,3584]{2,1,0:T(8,128)} %get-tuple-element.24.x_live, f32[2,8,3072]{2,1,0:T(8,128)} %get-tuple-element.25.x_dead, f32[2,8,3584]{2,1,0:T(8,128)} %get-tuple-element.26.r_live, f32[2,8,3072]{2,1,0:T(8,128)} %get-tuple-element.27.r_dead), custom_call_target="tpu_custom_call" | custom-call | tf_op jit(solution)/shard_map/unpack/pallas_call | solution.py:559

commit v2 on v1

v2 whole, which is shorter than its diff:
```python
import functools

import jax
import jax.numpy as jnp
from jax import lax
from jax.experimental import pallas as pl
from jax.experimental.pallas import tpu as pltpu
from jax.sharding import PartitionSpec as P

MESH = pl.DeviceIdType.MESH
F32 = jnp.float32
BF16 = jnp.bfloat16
VMEM_LIMIT = 56 * 1024 * 1024
NT = (((1,), (1,)), ((), ()))


def iota(shape, dim):
    return lax.broadcasted_iota(jnp.int32, shape, dim)


def tile_lanes(t, shift, less, tiles):
    at = lax.rem(t - shift // 128 - less + 2 * tiles, tiles) * 128
    return pl.ds(pl.multiple_of(at, 128), 128)


def rolled_tiles(load, shift, tiles, lane):
    within = lax.rem(shift, 128)
    before = pltpu.roll(load(tile_lanes(0, shift, 1, tiles)), within, 1)
    for t in range(tiles):
        now = pltpu.roll(load(tile_lanes(t, shift, 0, tiles)), within, 1)
        yield jnp.where(lane >= within, now, before)
        before = now


def pack_kernel(degrees, rows_step, orders, leg, rhs, guess, prior,
                leg_out, numbers, rhs_live, rhs_dead, x_live, x_dead, prior_live, prior_dead,
                mask, parity, rows_a, rows_b):
    pair = pl.program_id(0)
    block = pl.program_id(1)
    shift = orders[2 * pair]
    tiles = degrees // 128
    lane16 = iota((16, 128), 1)
    lane8 = iota((8, 128), 1)
    row8 = iota((8, 128), 0)

    def rows_of(step, carry):
        rows = pl.ds(pl.multiple_of(step * 16, 16), 16)
        moved = rolled_tiles(lambda at: leg[0, 1, rows, at], shift, tiles, lane16)
        for t, rolled in enumerate(moved):
            first = leg[0, 0, rows, t * 128:t * 128 + 128]
            kept = jnp.where(lane16 + t * 128 >= shift, first, rolled)
            leg_out[0, rows, t * 128:t * 128 + 128] = kept.astype(BF16)
        extra = jnp.where(lane16 == 0, pltpu.roll(rolled, 1, 1), jnp.zeros_like(rolled))
        leg_out[0, rows, degrees:degrees + 128] = extra.astype(BF16)
        return carry

    lax.fori_loop(0, rows_step // 16, rows_of, 0)

    @pl.when((pair == 0) & (block == 0))
    def _():
        tile = jnp.zeros((8, 128), jnp.int32)
        for m in range(8):
            tile = jnp.where(row8 == m, orders[m], tile)
        numbers[...] = tile

    for quad in range(2):
        @pl.when((pair == quad) & (block == 0))
        def _():
            upper = row8 < 4
            low, high = orders[4 * quad], orders[4 * quad + 2]
            shifts = jnp.where(upper, low, high)
            number_b = jnp.where(upper, orders[4 * quad + 1], orders[4 * quad + 3])
            tail = slice(degrees, degrees + 128)
            sources = [(rhs, rhs_live, rhs_dead), (guess, x_live, x_dead)]
            for at, (source, live, dead) in enumerate(sources):
                for half in range(2):
                    slot = 4 * quad + 2 * half
                    for r in range(2):
                        for c in range(2):
                            row = half * 4 + r * 2 + c
                            rows_a[at, row:row + 1, :] = source[r, c, slot:slot + 1, :]
                            rows_b[at, row:row + 1, :] = source[r, c, slot + 1:slot + 2, :]

            def both(load):
                for one, two in zip(rolled_tiles(load, low, tiles, lane8), rolled_tiles(load, high, tiles, lane8)):
                    yield jnp.where(upper, one, two)

            for at, (source, live, dead) in enumerate(sources):
                for t, rolled in enumerate(both(lambda lanes: rows_b[at, :, lanes])):
                    lanes = slice(t * 128, t * 128 + 128)
                    own = lane8 + t * 128 >= shifts
                    first = rows_a[at, :, lanes]
                    idle = jnp.where(own, rolled, first)
                    if t == tiles - 1:
                        idle = jnp.where(lane8 == 127, 0.0, idle)
                    live[quad, :, lanes] = jnp.where(own, first, rolled)
                    dead[quad, :, lanes] = idle
                live[quad, :, tail] = jnp.where(lane8 == 0, pltpu.roll(rolled, 1, 1), 0.0)
            for t, rolled in enumerate(both(lambda lanes: jnp.broadcast_to(prior[:, lanes], (8, 128)))):
                lanes = slice(t * 128, t * 128 + 128)
                place = lane8 + t * 128
                own = place >= shifts
                first = jnp.broadcast_to(prior[:, lanes], (8, 128))
                prior_live[quad, :, lanes] = jnp.where(own, first, rolled)
                prior_dead[quad, :, lanes] = jnp.where(own, rolled, first)
                total = jnp.where(own, place + shifts, place - shifts + degrees + number_b)
                parity[quad, :, lanes] = (1 - 2 * (total & 1)).astype(F32)
                mask[quad, :, lanes] = own.astype(F32)
            prior_live[quad, :, tail] = jnp.where(lane8 == 0, pltpu.roll(rolled, 1, 1), 0.0)
            parity[quad, :, tail] = jnp.ones((8, 128), F32)
            mask[quad, :, tail] = jnp.zeros((8, 128), F32)


def unpack_kernel(degrees, orders, x_live, x_dead, r_live, r_dead, x_out, r_out, rows_a, rows_b):
    tiles = degrees // 128
    lane8 = iota((8, 128), 1)
    upper = iota((8, 128), 0) < 4
    for quad in range(2):
        low, high = orders[4 * quad], orders[4 * quad + 2]
        shifts = jnp.where(upper, low, high)
        back_low, back_high = lax.rem(degrees - low, degrees), lax.rem(degrees - high, degrees)
        for at, (live, dead, out) in enumerate(((x_live, x_dead, x_out), (r_live, r_dead, r_out))):
            for t in range(tiles):
                lanes = slice(t * 128, t * 128 + 128)
                own = lane8 + t * 128 >= shifts
                alive, idle = live[quad, :, lanes], dead[quad, :, lanes]
                rows_a[at, :, lanes] = jnp.where(own, alive, idle)
                second = jnp.where(own, idle, alive)
                if t == tiles - 1:
                    extra = live[quad, :, degrees:degrees + 128]
                    second = jnp.where(lane8 == 127, pltpu.roll(extra, 127, 1), second)
                rows_b[at, :, lanes] = second
            load = lambda lanes: rows_b[at, :, lanes]
            back = zip(rolled_tiles(load, back_low, tiles, lane8), rolled_tiles(load, back_high, tiles, lane8))
            kept = [jnp.where(upper, one, two) for one, two in back]
            for t, value in enumerate(kept):
                rows_b[at, :, t * 128:t * 128 + 128] = value
            for half in range(2):
                slot = 4 * quad + 2 * half
                for r in range(2):
                    for c in range(2):
                        row = half * 4 + r * 2 + c
                        out[r, c, slot:slot + 1, :] = rows_a[at, row:row + 1, :]
                        out[r, c, slot + 1:slot + 2, :] = rows_b[at, row:row + 1, :]


def split_bf16(values):
    high = values.astype(BF16)
    return high, (values - high.astype(F32)).astype(BF16)


def main_kernel(n_order, n_blk, degrees, cycles, pixels,
                own_orders, leg_hbm, rhs_live_hbm, rhs_dead_hbm, x_live, x_dead_hbm, prior_live_hbm, prior_dead_hbm,
                mask, parity, noise_hbm, flags_hbm,
                x_out_live, x_out_dead, r_out_live, r_out_dead,
                leg, live, dead, rhs_live, rhs_dead, prior_live, prior_dead, noise, flags,
                lhs, modes, turned, back, send, recv, order_recv, scalar,
                flhs, weight, anal, sign, current, turn, table, sky_kept, pixel_sums,
                partial, extras, shard, rs_recv0, rs_recv1, summed, extra_sum,
                r1_live, r1_dead, steps,
                leg_sems, load_sems, order_sems, a2a_send, a2a_recv, rs_send, rs_arrive, ag_send, ag_arrive):
    me = lax.axis_index("order")
    mine = lax.axis_index("blk")
    tiles = degrees // 128
    half_turn = pixels // 2
    columns = 16 * n_order
    groups = columns // 128
    local = cycles * n_order
    part = degrees // n_blk
    sheets = modes.shape[0]

    def leg_copy(pair):
        return pltpu.make_async_copy(leg_hbm.at[pair], leg.at[pair], leg_sems.at[pair])

    def load_copy(at):
        source, target = ((x_dead_hbm, dead.at[0]), (prior_live_hbm, prior_live), (prior_dead_hbm, prior_dead),
                          (noise_hbm, noise), (flags_hbm, flags), (rhs_live_hbm, rhs_live),
                          (rhs_dead_hbm, rhs_dead))[at]
        return pltpu.make_async_copy(source, target, load_sems.at[at])

    for pair in range(4):
        leg_copy(pair).start()
    for at in range(7):
        load_copy(at).start()

    side_x = 2
    side_y = n_order // 4
    if n_order == 32:
        side_x, side_y = 4, 4
    offsets = [(a, b, c) for a in range(side_y) for b in range(side_x) for c in range(2) if a or b or c]
    offsets.sort(key=lambda o: -(2 * min(o[0], side_y - o[0]) + 2 * min(o[1], side_x - o[1]) + o[2]))
    my_y, my_x, my_c = me // (2 * side_x), (me // 2) % side_x, me % 2
    peers = [lax.rem(my_y + a, side_y) * (2 * side_x) + lax.rem(my_x + b, side_x) * 2 + lax.rem(my_c + c, 2)
             for a, b, c in offsets]
    steps_z = sorted(range(1, n_blk), key=lambda i: -min(i, n_blk - i))
    partners = [lax.rem(mine + i, n_blk) for i in steps_z]

    barrier = pltpu.get_barrier_semaphore()
    for to in peers:
        pl.semaphore_signal(barrier, inc=1, device_id=(to, mine), device_id_type=MESH)
    for to in partners:
        pl.semaphore_signal(barrier, inc=1, device_id=(me, to), device_id_type=MESH)

    def wait_bytes(ref, sem):
        pltpu.make_async_copy(ref, ref, sem).wait()

    row8 = iota((8, 128), 0)
    lane8 = iota((8, 128), 1)
    modes[...] = jnp.zeros_like(modes)
    turned[...] = jnp.zeros_like(turned)
    scalar[...] = jnp.zeros_like(scalar)
    pixel_sums[...] = jnp.zeros_like(pixel_sums)
    live[0] = x_live[...]

    pl.semaphore_wait(barrier, n_order - 1 + n_blk - 1)

    for to in peers:
        pltpu.make_async_remote_copy(
            src_ref=own_orders, dst_ref=order_recv.at[me],
            send_sem=order_sems.at[0], recv_sem=order_sems.at[1],
            device_id=(to, mine), device_id_type=MESH).start()
    order_recv[me] = own_orders[...]

    def exchange_start(step):
        for to in peers:
            pltpu.make_async_remote_copy(
                src_ref=send.at[to], dst_ref=recv.at[step, me],
                send_sem=a2a_send.at[step], recv_sem=a2a_recv.at[step],
                device_id=(to, mine), device_id_type=MESH).start()
        recv[step, me] = send[me]

    def exchange_wait(step):
        wait_bytes(recv.at[step, pl.ds(0, n_order - 1)], a2a_recv.at[step])
        wait_bytes(send.at[pl.ds(0, n_order - 1)], a2a_send.at[step])

    def build_weight():
        weight[...] = jnp.zeros_like(weight)
        for j in range(cycles):
            value = noise[j] * flags[j].astype(F32)
            for h in range(2):
                for image in range(2):
                    row = value[h:h + 1, image * half_turn:(image + 1) * half_turn]
                    for r in range(2):
                        weight[image * 4 + h * 2 + r, j:j + 1, :] = row

    def build_table():
        wait_bytes(order_recv.at[pl.ds(0, n_order - 1)], order_sems.at[1])
        wait_bytes(order_recv.at[pl.ds(0, n_order - 1)], order_sems.at[0])
        number = order_recv[...]
        lane = iota((n_order, 8, 128), 2)
        scale = jnp.where(number == 0, 1.0, 2.0) * (pixels ** -0.5)

        def angle(product):
            value = product.astype(F32)
            value = value - pixels * jnp.floor(value * (1.0 / pixels))
            return value * (2.0 * jnp.pi / pixels)

        base = angle(number * lane)
        current[:, 0] = scale * jnp.cos(base)
        current[:, 1] = -scale * jnp.sin(base)
        step = angle(number * 128)
        turn[:, 0] = jnp.cos(step)
        turn[:, 1] = jnp.sin(step)
        odd = (1 - 2 * (number & 1)).astype(F32)
        sign_rows = jnp.concatenate([odd, odd], axis=1).reshape(columns, 128)
        sign[...] = sign_rows.T[0:8]

        def block(q, carry):
            lanes = pl.ds(pl.multiple_of(q * 128, 128), 128)

            def some(piece, inner):
                for k in range(8):
                    s = piece * 8 + k
                    cosine, sine = current[s, 0], current[s, 1]
                    rows = pl.ds(pl.multiple_of(s * 16, 16), 16)
                    table[rows, lanes] = jnp.concatenate([cosine, sine], axis=0).astype(BF16)
                    turn_c, turn_s = turn[s, 0], turn[s, 1]
                    current[s, 0] = cosine * turn_c + sine * turn_s
                    current[s, 1] = sine * turn_c - cosine * turn_s
                return inner

            return lax.fori_loop(0, n_order // 8, some, carry)

        lax.fori_loop(0, half_turn // 128, block, 0)

    group8 = lane8 // 16
    item8 = lane8 // 8
    first_row8 = (iota((8, 1), 0) % 4) < 2

    def by_realization(total):
        zero = jnp.sum(jnp.where(first_row8, total, 0.0), axis=0, keepdims=True)
        one = jnp.sum(jnp.where(first_row8, 0.0, total), axis=0, keepdims=True)
        return [zero, one]

    def lane_sum(value):
        return jnp.sum(value, axis=1, keepdims=True)

    def put_scalars(values):
        tile = jnp.zeros((8, 128), F32)
        for at, value in enumerate(values):
            tile = jnp.where(item8 == at, value, tile)
        return tile

    def sum_tiles(load, count):
        values = [load(s) for s in range(count)]
        while len(values) > 1:
            values = [a + b for a, b in zip(values[::2], values[1::2])]
        return values[0]

    def scalar_at(total, row, at):
        return total[row:row + 1, 8 * at:8 * at + 1]

    def rows_from(pair):
        return jnp.where(first_row8, pair[0], pair[1])

    def pair_at(total, row, at):
        return [scalar_at(total, row, at), scalar_at(total, row, at + 1)]

    lane_step = 128 * max(n for n in (5, 3, 1) if (tiles + 1) % n == 0)
    width = degrees + 128

    def application(p, carry):
        for quad in range(2):
            @pl.when(p > 0)
            def _():
                wait_bytes(rs_recv0.at[p - 1, pl.ds(0, n_blk - 1)], ag_arrive.at[p - 1, quad])
                main = pl.ds(0, degrees)
                image = prior_live[quad, :, main] * live[p - 1, quad, :, main] + summed[p - 1, quad]
                live[p, quad, :, main] = jnp.where(p == 1, rhs_live[quad, :, main] - image, image)
                tail = pl.ds(degrees, 128)
                image = prior_live[quad, :, tail] * live[p - 1, quad, :, tail] + extra_sum[quad]
                live[p, quad, :, tail] = jnp.where(p == 1, rhs_live[quad, :, tail] - image, image)

            def build(t, inner_carry):
                at = pl.ds(pl.multiple_of(t * lane_step, 128), lane_step)
                value = live[p, quad, :, at]
                first = mask[quad, :, at]
                second = 1.0 - first
                flip = parity[quad, :, at]
                high = value.astype(BF16).astype(F32)
                rest = value - high
                pieces = []
                for piece in (high, rest):
                    for keep in (first, second):
                        kept = piece * keep
                        pieces.append(kept)
                        pieces.append(kept * flip)
                lhs[quad, :, at] = jnp.concatenate(pieces, axis=0).astype(BF16)
                return inner_carry

            lax.fori_loop(0, width // lane_step, build, 0)
            for half in range(2):
                pair = 2 * quad + half

                @pl.when(p == 0)
                def _():
                    leg_copy(pair).wait()

                out = lax.dot_general(lhs[quad], leg[pair], NT, preferred_element_type=F32)
                out = out[0:32] + out[32:64]
                at = 4 * half
                for slot in range(2):
                    rows = jnp.concatenate([out[16 * slot + at:16 * slot + at + 4],
                                            out[16 * slot + 8 + at:16 * slot + 8 + at + 4]], axis=0)
                    if sheets * 128 > local:
                        rows = jnp.concatenate([rows, jnp.zeros((8, sheets * 128 - local), F32)], axis=1)
                    for sheet in range(sheets):
                        modes[sheet, pl.ds(2 * pair + slot, 8, stride=8), :] = rows[:, 128 * sheet:128 * sheet + 128]

        @pl.when(p > 0)
        def _():
            for quad in range(2):
                wait_bytes(rs_recv0.at[p - 1, pl.ds(0, n_blk - 1)], ag_send.at[p - 1, quad])

        for sheet in range(sheets):
            turned[128 * sheet:128 * sheet + 128, :] = modes[sheet].T

        @pl.when(p == 2)
        def _():
            norm = cross = jnp.zeros((8, 1), F32)
            for quad in range(2):
                for held in (live, dead):
                    norm = norm + lane_sum(held[1, quad] * held[1, quad])
                    cross = cross + lane_sum(held[1, quad] * held[2, quad])
            scalar[...] = put_scalars(by_realization(norm) + by_realization(cross))

        for d in range(n_order):
            send[d] = jnp.where(row8 < cycles, turned[cycles * d:cycles * d + 8, :], scalar[...])
        exchange_start(2 * p)

        @pl.when(p == 0)
        def _():
            build_table()
            load_copy(3).wait()
            load_copy(4).wait()
            build_weight()

        exchange_wait(2 * p)

        @pl.when(p == 2)
        def _():
            total = sum_tiles(lambda s: recv[2 * p, s], n_order)
            norm, cross = pair_at(total, 7, 0), pair_at(total, 7, 2)
            ratio = [norm[0] / cross[0], norm[1] / cross[1]]
            step = rows_from(ratio)
            steps[0] = jnp.broadcast_to(rows_from(norm), (8, 128))
            steps[1] = jnp.broadcast_to(step, (8, 128))
            steps[2] = jnp.broadcast_to(ratio[0], (8, 128))
            steps[3] = jnp.broadcast_to(ratio[1], (8, 128))
            sums = [jnp.zeros((8, 1), F32)] * 4
            for quad in range(2):
                for r1, held, inv in ((r1_live, live, prior_live), (r1_dead, dead, prior_dead)):
                    before = held[1, quad]
                    after = before - step * held[2, quad]
                    r1[quad] = after
                    scaled = inv[quad] * after
                    sums = [total + lane_sum(value) for total, value in zip(
                        sums, (after * after, scaled * after, scaled * before, inv[quad] * before * before))]
            scalar[...] = put_scalars([value for total in sums for value in by_realization(total)])

        def shuffle(g, inner_carry):
            lanes = pl.ds(pl.multiple_of(g * 128, 128), 128)
            flip = sign[:, lanes]
            held = [recv[2 * p, g * 8 + i] for i in range(8)]
            straight = []
            for hr in range(4):
                acc = held[0] if hr == 0 else pltpu.roll(held[0], (128 - 16 * hr) % 128, 1)
                for i in range(1, 8):
                    by = (16 * i - 16 * hr) % 128
                    moved = held[i] if by == 0 else pltpu.roll(held[i], by, 1)
                    acc = jnp.where(group8 == i, moved, acc)
                straight.append(acc)
            flipped = [acc * flip for acc in straight]
            rows = jnp.concatenate(straight + flipped, axis=0)
            high, rest = split_bf16(rows)
            flhs[0:64, lanes] = high
            flhs[64:128, lanes] = rest
            return inner_carry

        lax.fori_loop(0, groups, shuffle, 0)

        anal[...] = jnp.zeros_like(anal)
        chunk = min(512, half_turn)

        def fourier(t, inner_carry):
            lanes = pl.ds(pl.multiple_of(t * chunk, 128), chunk)
            block = table[:, lanes]
            sky = jnp.dot(flhs[...], block, preferred_element_type=F32)
            sky = sky[0:64] + sky[64:128]
            scaled = sky * weight[:, :, lanes].reshape(64, chunk)
            high, rest = split_bf16(scaled)
            out = lax.dot_general(jnp.concatenate([high, rest], axis=0), block, NT, preferred_element_type=F32)
            anal[...] += out[0:64] + out[64:128]

            @pl.when(p == 1)
            def _():
                sky_kept[:, lanes] = sky

            @pl.when(p == 2)
            def _():
                for hr in range(8):
                    rows = slice(8 * hr, 8 * hr + 8)
                    before = sky_kept[rows, lanes]
                    after = before - steps[2 + hr % 2][:, 0:1] * sky[rows]
                    weighed = weight[hr, :, lanes]
                    heavy = weighed * after
                    for at, value in enumerate((heavy * after, heavy * before, weighed * before * before)):
                        total = pixel_sums[2 * at + hr % 2]
                        for k in range(chunk // 128):
                            total = total + value[:, 128 * k:128 * k + 128]
                        pixel_sums[2 * at + hr % 2] = total

            return inner_carry

        lax.fori_loop(0, half_turn // chunk, fourier, 0)

        @pl.when(p == 2)
        def _():
            tile = scalar[...]
            for at in range(6):
                value = jnp.sum(lane_sum(pixel_sums[at]), axis=0, keepdims=True)
                tile = jnp.where(item8 == 8 + at, value, tile)
            scalar[...] = tile

        def shuffle_back(g, inner_carry):
            lanes = pl.ds(pl.multiple_of(g * 128, 128), 128)
            flip = sign[:, lanes]
            rows = [anal[8 * hr:8 * hr + 8, lanes] + flip * anal[32 + 8 * hr:40 + 8 * hr, lanes] for hr in range(4)]
            base = scalar[...]
            for i in range(8):
                acc = jnp.zeros((8, 128), F32)
                for hr in range(4):
                    by = (16 * hr - 16 * i) % 128
                    moved = rows[hr] if by == 0 else pltpu.roll(rows[hr], by, 1)
                    acc = jnp.where(group8 == hr, moved, acc)
                send[g * 8 + i] = jnp.where(row8 < cycles, acc, base)
            return inner_carry

        lax.fori_loop(0, groups, shuffle_back, 0)
        exchange_start(2 * p + 1)

        @pl.when(p == 0)
        def _():
            for at in (0, 1, 2, 5, 6):
                load_copy(at).wait()

        for quad in range(2):
            image = prior_dead[quad] * dead[p, quad]
            dead[p + 1, quad] = jnp.where(p == 0, rhs_dead[quad] - image, image)
        exchange_wait(2 * p + 1)

        for d in range(n_order):
            turned[cycles * d:cycles * d + cycles, :] = recv[2 * p + 1, d, 0:cycles, :]
        for sheet in range(sheets):
            back[sheet] = turned[128 * sheet:128 * sheet + 128, :].T

        for quad in range(2):
            for half in range(2):
                pair = 2 * quad + half
                rows = jnp.concatenate([
                    jnp.concatenate([back[sheet, pl.ds(2 * pair + slot, 8, stride=8), :] for sheet in range(sheets)],
                                    axis=1)
                    for slot in range(2)], axis=0)
                high, rest = split_bf16(rows[:, 0:local])
                both = jnp.concatenate([high, rest], axis=0)
                mine_rows = slice(4 * half, 4 * half + 4)
                one_row = slice(4 * half, 4 * half + 1)

                def analyse(t, inner_carry):
                    at = pl.ds(pl.multiple_of(t * 2 * part, 128), 2 * part)
                    out = jnp.dot(both, leg[pair, :, at], preferred_element_type=F32)
                    out = out[0:16] + out[16:32]
                    kept = jnp.where(mask[quad, one_row, at] > 0.5, out[0:8], out[8:16])
                    value = kept[0:4] + parity[quad, one_row, at] * kept[4:8]
                    partial[quad, 2 * t, mine_rows, 0:part] = value[:, 0:part]
                    partial[quad, 2 * t + 1, mine_rows, 0:part] = value[:, part:2 * part]
                    return inner_carry

                lax.fori_loop(0, n_blk // 2, analyse, 0)
                out = jnp.dot(both, leg[pair, :, degrees:degrees + 128], preferred_element_type=F32)
                out = out[0:16] + out[16:32]
                extras[quad, mine_rows, :] = out[8:12] + out[12:16]
            if quad == 1:
                total = sum_tiles(lambda s: recv[2 * p + 1, s], n_order)
                tile = jnp.where(lane8 == 0, extras[0], 0.0)
                tile = jnp.where(lane8 == 1, pltpu.roll(extras[1], 1, 1), tile)
                scalar[...] = total
                tile = jnp.where((lane8 >= 64) & (row8 == 7), total, tile)
                for b in range(n_blk):
                    partial[1, b, :, part:part + 128] = tile
            for to in partners:
                source = partial.at[0, to, :, pl.ds(0, part)] if quad == 0 else partial.at[1, to]
                target = rs_recv0 if quad == 0 else rs_recv1
                pltpu.make_async_remote_copy(
                    src_ref=source, dst_ref=target.at[p, mine],
                    send_sem=rs_send.at[p, quad], recv_sem=rs_arrive.at[p, quad],
                    device_id=(me, to), device_id_type=MESH).start()

        my_lanes = pl.ds(pl.multiple_of(mine * part, 128), part)
        for quad in range(2):
            arrived = rs_recv0 if quad == 0 else rs_recv1
            arrived[p, mine] = partial[quad, mine, :, 0:arrived.shape[3]]
            wait_bytes(arrived.at[p, pl.ds(0, n_blk - 1)], rs_arrive.at[p, quad])
            total = sum_tiles(lambda b: arrived[p, b], n_blk)
            shard[quad] = total[:, 0:part]
            for to in partners:
                pltpu.make_async_remote_copy(
                    src_ref=shard.at[quad], dst_ref=summed.at[p, quad, :, my_lanes],
                    send_sem=ag_send.at[p, quad], recv_sem=ag_arrive.at[p, quad],
                    device_id=(me, to), device_id_type=MESH).start()
            summed[p, quad, :, my_lanes] = total[:, 0:part]
            wait_bytes(arrived.at[p, pl.ds(0, n_blk - 1)], rs_send.at[p, quad])
        tile = total[:, part:part + 128]
        extra_sum[0] = jnp.where(lane8 == 0, tile, 0.0)
        extra_sum[1] = jnp.where(lane8 == 0, pltpu.roll(tile, 127, 1), 0.0)
        extra_sum[2] = tile
        return carry

    lax.fori_loop(0, 3, application, 0)

    within_order, over_all = scalar[...], extra_sum[2]
    norm = [steps[0, 0:1, 0:1], steps[0, 2:3, 0:1]]
    ratios, seconds = [], []
    for r in range(2):
        after = scalar_at(within_order, 7, r)
        ratio = after / norm[r]
        curve = (scalar_at(within_order, 7, 2 + r) + scalar_at(over_all, 7, 8 + r)
                 + 2.0 * ratio * (scalar_at(within_order, 7, 4 + r) + scalar_at(over_all, 7, 10 + r))
                 + ratio * ratio * (scalar_at(within_order, 7, 6 + r) + scalar_at(over_all, 7, 12 + r)))
        ratios.append(ratio)
        seconds.append(after / curve)
    ratio, second = rows_from(ratios), rows_from(seconds)
    step = steps[1, :, 0:1]

    def finish(quad, lanes, held, r1, last, x_out, r_out):
        before, middle = held[1, quad, :, lanes], held[2, quad, :, lanes]
        after = r1[quad, :, lanes]
        direction = after + ratio * before
        image = (1.0 + ratio) * middle - step * last
        x_out[quad, :, lanes] = held[0, quad, :, lanes] + step * before + second * direction
        r_out[quad, :, lanes] = after - second * image

    main, tail = pl.ds(0, degrees), pl.ds(degrees, 128)
    for quad in range(2):
        finish(quad, main, dead, r1_dead, dead[3, quad], x_out_dead, r_out_dead)
        last = prior_live[quad, :, tail] * live[2, quad, :, tail] + extra_sum[quad]
        finish(quad, tail, live, r1_live, last, x_out_live, r_out_live)
    for quad in range(2):
        wait_bytes(rs_recv0.at[2, pl.ds(0, n_blk - 1)], ag_arrive.at[2, quad])
        last = prior_live[quad, :, main] * live[2, quad, :, main] + summed[2, quad]
        finish(quad, main, live, r1_live, last, x_out_live, r_out_live)
    for quad in range(2):
        wait_bytes(rs_recv0.at[2, pl.ds(0, n_blk - 1)], ag_send.at[2, quad])


def per_device(n_order, n_blk, right_side, start_guess, legendre, orders, prior_inv, noise_inv, pixel_flags):
    slots, local, degrees = legendre.shape
    cycles, pixels = noise_inv.shape[1], noise_inv.shape[2]
    width = degrees + 128
    part = degrees // n_blk
    smem = pl.BlockSpec(memory_space=pltpu.SMEM)
    vmem = pl.BlockSpec(memory_space=pltpu.VMEM)
    hbm = pl.BlockSpec(memory_space=pl.ANY)
    live_shape = jax.ShapeDtypeStruct((2, 8, width), F32)
    dead_shape = jax.ShapeDtypeStruct((2, 8, degrees), F32)
    columns = 16 * n_order
    sheets = -(-(local + 8) // 128)
    half_turn = pixels // 2
    rows_step = local // 2 if (local // 2) % 16 == 0 else local
    packed = pl.pallas_call(
        functools.partial(pack_kernel, degrees, rows_step),
        grid=(4, local // rows_step),
        in_specs=[smem, pl.BlockSpec((1, 2, rows_step, degrees), lambda k, b: (k, 0, b, 0)), vmem, vmem, vmem],
        out_specs=[pl.BlockSpec((1, rows_step, width), lambda k, b: (k, b, 0))] + [vmem] * 9,
        out_shape=[jax.ShapeDtypeStruct((4, local, width), BF16), jax.ShapeDtypeStruct((8, 128), jnp.int32)]
        + [live_shape, dead_shape] * 3 + [live_shape] * 2,
        scratch_shapes=[pltpu.VMEM((2, 8, degrees), F32)] * 2,
        compiler_params=pltpu.CompilerParams(vmem_limit_bytes=VMEM_LIMIT),
        name="pack",
    )(orders, legendre.reshape(4, 2, local, degrees), right_side, start_guess, prior_inv.reshape(1, degrees))
    leg, numbers, rhs_live, rhs_dead, x_live, x_dead, prior_live, prior_dead, mask, parity = packed

    scratch = [
        pltpu.VMEM((4, local, width), BF16),
        pltpu.VMEM((3, 2, 8, width), F32),
        pltpu.VMEM((4, 2, 8, degrees), F32),
        pltpu.VMEM((2, 8, width), F32),
        pltpu.VMEM((2, 8, degrees), F32),
        pltpu.VMEM((2, 8, width), F32),
        pltpu.VMEM((2, 8, degrees), F32),
        pltpu.VMEM((cycles, 2, pixels), F32),
        pltpu.VMEM((cycles, 2, pixels), jnp.int32),
        pltpu.VMEM((2, 64, width), BF16),
        pltpu.VMEM((sheets, 128, 128), F32),
        pltpu.VMEM((sheets * 128, 128), F32),
        pltpu.VMEM((sheets, 128, 128), F32),
        pltpu.VMEM((n_order, 8, 128), F32),
        pltpu.VMEM((6, n_order, 8, 128), F32),
        pltpu.VMEM((n_order, 8, 128), jnp.int32),
        pltpu.VMEM((8, 128), F32),
        pltpu.VMEM((128, columns), BF16),
        pltpu.VMEM((8, 8, half_turn), F32),
        pltpu.VMEM((64, columns), F32),
        pltpu.VMEM((8, columns), F32),
        pltpu.VMEM((n_order, 2, 8, 128), F32),
        pltpu.VMEM((n_order, 2, 8, 128), F32),
        pltpu.VMEM((columns, half_turn), BF16),
        pltpu.VMEM((64, half_turn), F32),
        pltpu.VMEM((6, 8, 128), F32),
        pltpu.VMEM((2, n_blk, 8, part + 128), F32),
        pltpu.VMEM((2, 8, 128), F32),
        pltpu.VMEM((2, 8, part), F32),
        pltpu.VMEM((3, n_blk, 8, part), F32),
        pltpu.VMEM((3, n_blk, 8, part + 128), F32),
        pltpu.VMEM((3, 2, 8, degrees), F32),
        pltpu.VMEM((3, 8, 128), F32),
        pltpu.VMEM((2, 8, width), F32),
        pltpu.VMEM((2, 8, degrees), F32),
        pltpu.VMEM((4, 8, 128), F32),
        pltpu.SemaphoreType.DMA((4,)),
        pltpu.SemaphoreType.DMA((7,)),
        pltpu.SemaphoreType.DMA((2,)),
        pltpu.SemaphoreType.DMA((6,)),
        pltpu.SemaphoreType.DMA((6,)),
        pltpu.SemaphoreType.DMA((3, 2)),
        pltpu.SemaphoreType.DMA((3, 2)),
        pltpu.SemaphoreType.DMA((3, 2)),
        pltpu.SemaphoreType.DMA((3, 2)),
    ]
    results = pl.pallas_call(
        functools.partial(main_kernel, n_order, n_blk, degrees, cycles, pixels),
        in_specs=[vmem, hbm, hbm, hbm, vmem, hbm, hbm, hbm, vmem, vmem, hbm, hbm],
        out_specs=[vmem] * 4,
        out_shape=[live_shape, dead_shape, live_shape, dead_shape],
        scratch_shapes=scratch,
        compiler_params=pltpu.CompilerParams(
            collective_id=0, has_side_effects=True, vmem_limit_bytes=VMEM_LIMIT),
        name="steps",
    )(numbers, leg, rhs_live, rhs_dead, x_live, x_dead, prior_live, prior_dead, mask, parity,
      noise_inv.transpose(1, 0, 2), pixel_flags.transpose(1, 0, 2))

    full = jax.ShapeDtypeStruct(right_side.shape, F32)
    return tuple(pl.pallas_call(
        functools.partial(unpack_kernel, degrees),
        in_specs=[smem] + [vmem] * 4,
        out_specs=[vmem] * 2,
        out_shape=[full, full],
        scratch_shapes=[pltpu.VMEM((2, 8, degrees), F32)] * 2,
        compiler_params=pltpu.CompilerParams(vmem_limit_bytes=VMEM_LIMIT),
        name="unpack",
    )(orders, *results))


def solution(mesh):
    in_specs = (
        P(None, None, "order", None),
        P(None, None, "order", None),
        P("order", "blk", None),
        P("order"),
        P(),
        P(None, ("blk", "order"), None),
        P(None, ("blk", "order"), None),
    )
    out_specs = (P(None, None, "order", None), P(None, None, "order", None))
    body = functools.partial(per_device, mesh.shape["order"], mesh.shape["blk"])
    return jax.shard_map(body, mesh=mesh, in_specs=in_specs, out_specs=out_specs, check_vma=False)
```

time: 157 us -> 121 us (0.77)
  Pallas kernels: 151 us -> 120 us
  local copies, waits for them, and re-layouts: 5.09 us -> 0 us
    pallas_call x1, Pallas kernels: 132 us -> 103 us  [per_device(): pl.pallas_call(functools.partial(main_kernel, n_order, n_blk, degrees, cy...]
    unnamed x2 -> x0, local copies, waits for them, and re-layouts: 3.77 us -> none
    pallas_call x1, Pallas kernels: 15.5 us -> 13.7 us  [per_device(): pl.pallas_call(functools.partial(pack_kernel, degrees, rows_step), grid=(...]
where the time goes in v2:
time: 121 us; the launch traced here: 120 us
  Pallas kernels  120 us (99%)
    pallas_call x1, Pallas kernels, per_device(): pl.pallas_call(functools.partial(main_kernel, n_order, n_blk, degrees, cy...  103 us
    pallas_call x1, Pallas kernels, per_device(): pl.pallas_call(functools.partial(pack_kernel, degrees, rows_step), grid=(...  13.7 us
    pallas_call x1, Pallas kernels, per_device(): pl.pallas_call(functools.partial(unpack_kernel, degrees), in_specs=[smem]...  2.89 us

profile of v2, /device:TPU:1, one launch (start us, length us, event | category | flops | bytes accessed | tf_op | source)
XLA Modules:
  0.0 120.3 jit_solution(5166278150594501631)
XLA Ops:
  0.6 13.7 %pack.1 = (bf16[4,192,3200]{2,1,0:T(8,128)(2,1)}, s32[8,128]{1,0:T(8,128)}, f32[2,8,3200]{2,1,0:T(8,128)}, f32[2,8,3072]{2,1,0:T(8,128)}, f32[2,8,3200]{2,1,0:T(...) custom-call(s32[8]{0:T(128)} %orders.3, ...), custom_call_target="tpu_custom_call" | custom-call | tf_op jit(solution)/shard_map/pack/pallas_call | solution.py:630
  14.4 103.1 %steps.1 = (f32[2,8,3200]{2,1,0:T(8,128)}, f32[2,8,3072]{2,1,0:T(8,128)}, f32[2,8,3200]{2,1,0:T(8,128)}, f32[2,8,3072]{2,1,0:T(8,128)}) custom-call(s32[8,128]{1,0:T(8,128)} %get-tuple-element.16.own_orders, bf16[4,192,3200]{2,1,0:T(8,128)(2,1)} %get-tuple-element.17.leg_hbm, f32[2,8,3200]{2,1,0:T(8,128)} %get-tuple-element.18.rhs_live_hbm, ...), custom_call_target="tpu_custom_call" | custom-call | tf_op jit(solution)/shard_map/steps/pallas_call | solution.py:690
  117.5 2.9 %unpack.1 = (f32[2,2,8,3072]{3,2,1,0:T(8,128)}, f32[2,2,8,3072]{3,2,1,0:T(8,128)}) custom-call(s32[8]{0:T(128)} %orders.3, f32[2,8,3200]{2,1,0:T(8,128)} %get-tuple-element.26.x_live, f32[2,8,3072]{2,1,0:T(8,128)} %get-tuple-element.27.x_dead, f32[2,8,3200]{2,1,0:T(8,128)} %get-tuple-element.28.r_live, f32[2,8,3072]{2,1,0:T(8,128)} %get-tuple-element.29.r_dead), custom_call_target="tpu_custom_call" | custom-call | tf_op jit(solution)/shard_map/unpack/pallas_call | solution.py:703

commit v3 on v2

--- a/solution.py
+++ b/solution.py
@@ -11,6 +11,7 @@
 F32 = jnp.float32
 BF16 = jnp.bfloat16
 VMEM_LIMIT = 56 * 1024 * 1024
+PACK_VMEM = 56 * 1024 * 1024
 NT = (((1,), (1,)), ((), ()))
 
 
@@ -32,83 +33,103 @@
         before = now
 
 
-def pack_kernel(degrees, rows_step, orders, leg, rhs, guess, prior,
+def pack_kernel(degrees, span, orders, leg_hbm, rhs, guess, prior,
                 leg_out, numbers, rhs_live, rhs_dead, x_live, x_dead, prior_live, prior_dead,
-                mask, parity, rows_a, rows_b):
-    pair = pl.program_id(0)
-    block = pl.program_id(1)
-    shift = orders[2 * pair]
+                mask, parity, stage, packed, rows_a, rows_b, in_sems, out_sems):
     tiles = degrees // 128
+    blocks = tiles // span
+    local = packed.shape[1]
     lane16 = iota((16, 128), 1)
     lane8 = iota((8, 128), 1)
     row8 = iota((8, 128), 0)
-
-    def rows_of(step, carry):
-        rows = pl.ds(pl.multiple_of(step * 16, 16), 16)
-        moved = rolled_tiles(lambda at: leg[0, 1, rows, at], shift, tiles, lane16)
-        for t, rolled in enumerate(moved):
-            first = leg[0, 0, rows, t * 128:t * 128 + 128]
-            kept = jnp.where(lane16 + t * 128 >= shift, first, rolled)
-            leg_out[0, rows, t * 128:t * 128 + 128] = kept.astype(BF16)
-        extra = jnp.where(lane16 == 0, pltpu.roll(rolled, 1, 1), jnp.zeros_like(rolled))
-        leg_out[0, rows, degrees:degrees + 128] = extra.astype(BF16)
-        return carry
-
-    lax.fori_loop(0, rows_step // 16, rows_of, 0)
-
-    @pl.when((pair == 0) & (block == 0))
-    def _():
-        tile = jnp.zeros((8, 128), jnp.int32)
-        for m in range(8):
-            tile = jnp.where(row8 == m, orders[m], tile)
-        numbers[...] = tile
-
+    upper = row8 < 4
+
+    for pair in range(4):
+        own_blocks = orders[2 * pair] // (128 * span)
+        for j in range(blocks + 1):
+            second = j <= own_blocks
+            slot = 2 * pair + jnp.where(second, 1, 0)
+            column = jnp.where(second, blocks - 1 - own_blocks + j, j - 1) * (128 * span)
+            lanes = pl.ds(pl.multiple_of(column, 128), 128 * span)
+            pltpu.make_async_copy(leg_hbm.at[slot, :, lanes],
+                                  stage.at[pair, :, pl.ds(j * 128 * span, 128 * span)], in_sems.at[pair]).start()
+
+    tile = jnp.zeros((8, 128), jnp.int32)
+    for m in range(8):
+        tile = jnp.where(row8 == m, orders[m], tile)
+    numbers[...] = tile
+    tail = slice(degrees, degrees + 128)
+    sources = [(rhs, rhs_live, rhs_dead), (guess, x_live, x_dead)]
     for quad in range(2):
-        @pl.when((pair == quad) & (block == 0))
-        def _():
-            upper = row8 < 4
-            low, high = orders[4 * quad], orders[4 * quad + 2]
-            shifts = jnp.where(upper, low, high)
-            number_b = jnp.where(upper, orders[4 * quad + 1], orders[4 * quad + 3])
-            tail = slice(degrees, degrees + 128)
-            sources = [(rhs, rhs_live, rhs_dead), (guess, x_live, x_dead)]
-            for at, (source, live, dead) in enumerate(sources):
-                for half in range(2):
-                    slot = 4 * quad + 2 * half
-                    for r in range(2):
-                        for c in range(2):
-                            row = half * 4 + r * 2 + c
-                            rows_a[at, row:row + 1, :] = source[r, c, slot:slot + 1, :]
-                            rows_b[at, row:row + 1, :] = source[r, c, slot + 1:slot + 2, :]
-
-            def both(load):
-                for one, two in zip(rolled_tiles(load, low, tiles, lane8), rolled_tiles(load, high, tiles, lane8)):
-                    yield jnp.where(upper, one, two)
-
-            for at, (source, live, dead) in enumerate(sources):
-                for t, rolled in enumerate(both(lambda lanes: rows_b[at, :, lanes])):
-                    lanes = slice(t * 128, t * 128 + 128)
-                    own = lane8 + t * 128 >= shifts
-                    first = rows_a[at, :, lanes]
-                    idle = jnp.where(own, rolled, first)
-                    if t == tiles - 1:
-                        idle = jnp.where(lane8 == 127, 0.0, idle)
-                    live[quad, :, lanes] = jnp.where(own, first, rolled)
-                    dead[quad, :, lanes] = idle
-                live[quad, :, tail] = jnp.where(lane8 == 0, pltpu.roll(rolled, 1, 1), 0.0)
-            for t, rolled in enumerate(both(lambda lanes: jnp.broadcast_to(prior[:, lanes], (8, 128)))):
+        low, high = orders[4 * quad], orders[4 * quad + 2]
+        shifts = jnp.where(upper, low, high)
+        number_b = jnp.where(upper, orders[4 * quad + 1], orders[4 * quad + 3])
+        for at, (source, live, dead) in enumerate(sources):
+            for half in range(2):
+                slot = 4 * quad + 2 * half
+                for r in range(2):
+                    for c in range(2):
+                        row = half * 4 + r * 2 + c
+                        rows_a[quad, at, row:row + 1, :] = source[r, c, slot:slot + 1, :]
+                        rows_b[quad, at, row:row + 1, :] = source[r, c, slot + 1:slot + 2, :]
+
+        def both(load):
+            for one, two in zip(rolled_tiles(load, low, tiles, lane8), rolled_tiles(load, high, tiles, lane8)):
+                yield jnp.where(upper, one, two)
+
+        for at, (source, live, dead) in enumerate(sources):
+            for t, rolled in enumerate(both(lambda lanes: rows_b[quad, at, :, lanes])):
                 lanes = slice(t * 128, t * 128 + 128)
-                place = lane8 + t * 128
-                own = place >= shifts
-                first = jnp.broadcast_to(prior[:, lanes], (8, 128))
-                prior_live[quad, :, lanes] = jnp.where(own, first, rolled)
-                prior_dead[quad, :, lanes] = jnp.where(own, rolled, first)
-                total = jnp.where(own, place + shifts, place - shifts + degrees + number_b)
-                parity[quad, :, lanes] = (1 - 2 * (total & 1)).astype(F32)
-                mask[quad, :, lanes] = own.astype(F32)
-            prior_live[quad, :, tail] = jnp.where(lane8 == 0, pltpu.roll(rolled, 1, 1), 0.0)
-            parity[quad, :, tail] = jnp.ones((8, 128), F32)
-            mask[quad, :, tail] = jnp.zeros((8, 128), F32)
+                own = lane8 + t * 128 >= shifts
+                first = rows_a[quad, at, :, lanes]
+                idle = jnp.where(own, rolled, first)
+                if t == tiles - 1:
+                    idle = jnp.where(lane8 == 127, 0.0, idle)
+                live[quad, :, lanes] = jnp.where(own, first, rolled)
+                dead[quad, :, lanes] = idle
+            live[quad, :, tail] = jnp.where(lane8 == 0, pltpu.roll(rolled, 1, 1), 0.0)
+        for t, rolled in enumerate(both(lambda lanes: jnp.broadcast_to(prior[:, lanes], (8, 128)))):
+            lanes = slice(t * 128, t * 128 + 128)
+            place = lane8 + t * 128
+            own = place >= shifts
+            first = jnp.broadcast_to(prior[:, lanes], (8, 128))
+            prior_live[quad, :, lanes] = jnp.where(own, first, rolled)
+            prior_dead[quad, :, lanes] = jnp.where(own, rolled, first)
+            total = jnp.where(own, place + shifts, place - shifts + degrees + number_b)
+            parity[quad, :, lanes] = (1 - 2 * (total & 1)).astype(F32)
+            mask[quad, :, lanes] = own.astype(F32)
+        prior_live[quad, :, tail] = jnp.where(lane8 == 0, pltpu.roll(rolled, 1, 1), 0.0)
+        parity[quad, :, tail] = jnp.ones((8, 128), F32)
+        mask[quad, :, tail] = jnp.zeros((8, 128), F32)
+
+    for pair in range(4):
+        shift = orders[2 * pair]
+        within = lax.rem(shift, 128)
+        back = span - 1 - lax.rem(shift // 128, span)
+        pltpu.make_async_copy(stage.at[pair], stage.at[pair], in_sems.at[pair]).wait()
+
+        def rows_of(step, carry):
+            rows = pl.ds(pl.multiple_of(step * 16, 16), 16)
+
+            def moved(t):
+                lanes = pl.ds(pl.multiple_of((t + back) * 128, 128), 128)
+                return pltpu.roll(stage[pair, rows, lanes], within, 1)
+
+            before = moved(0)
+            extra = jnp.where(lane16 == 0, pltpu.roll(before, 1, 1), jnp.zeros_like(before))
+            packed[pair, rows, degrees:degrees + 128] = extra
+            for t in range(tiles):
+                now = moved(t + 1)
+                rolled = jnp.where(lane16 >= within, now, before)
+                first = stage[pair, rows, (t + span) * 128:(t + span) * 128 + 128]
+                packed[pair, rows, t * 128:t * 128 + 128] = jnp.where(lane16 + t * 128 >= shift, first, rolled)
+                before = now
+            return carry
+
+        lax.fori_loop(0, local // 16, rows_of, 0, unroll=4 if local % 64 == 0 else 1)
+        pltpu.make_async_copy(packed.at[pair], leg_out.at[pair], out_sems.at[pair]).start()
+    for pair in range(4):
+        pltpu.make_async_copy(packed.at[pair], leg_out.at[pair], out_sems.at[pair]).wait()
 
 
 def unpack_kernel(degrees, orders, x_live, x_dead, r_live, r_dead, x_out, r_out, rows_a, rows_b):
@@ -332,7 +353,7 @@
                 live[p, quad, :, tail] = jnp.where(p == 1, rhs_live[quad, :, tail] - image, image)
 
             def build(t, inner_carry):
-                at = pl.ds(pl.multiple_of(t * lane_step, 128), lane_step)
+                at = pl.ds(t * lane_step, lane_step)
                 value = live[p, quad, :, at]
                 first = mask[quad, :, at]
                 second = 1.0 - first
@@ -348,7 +369,8 @@
                 lhs[quad, :, at] = jnp.concatenate(pieces, axis=0).astype(BF16)
                 return inner_carry
 
-            lax.fori_loop(0, width // lane_step, build, 0)
+            for t in range(width // lane_step):
+                build(t, 0)
             for half in range(2):
                 pair = 2 * quad + half
 
@@ -419,7 +441,7 @@
             scalar[...] = put_scalars([value for total in sums for value in by_realization(total)])
 
         def shuffle(g, inner_carry):
-            lanes = pl.ds(pl.multiple_of(g * 128, 128), 128)
+            lanes = pl.ds(g * 128, 128)
             flip = sign[:, lanes]
             held = [recv[2 * p, g * 8 + i] for i in range(8)]
             straight = []
@@ -437,10 +459,11 @@
             flhs[64:128, lanes] = rest
             return inner_carry
 
-        lax.fori_loop(0, groups, shuffle, 0)
+        for g in range(groups):
+            shuffle(g, 0)
 
         anal[...] = jnp.zeros_like(anal)
-        chunk = min(512, half_turn)
+        chunk = min(1536, half_turn)
 
         def fourier(t, inner_carry):
             lanes = pl.ds(pl.multiple_of(t * chunk, 128), chunk)
@@ -483,7 +506,7 @@
             scalar[...] = tile
 
         def shuffle_back(g, inner_carry):
-            lanes = pl.ds(pl.multiple_of(g * 128, 128), 128)
+            lanes = pl.ds(g * 128, 128)
             flip = sign[:, lanes]
             rows = [anal[8 * hr:8 * hr + 8, lanes] + flip * anal[32 + 8 * hr:40 + 8 * hr, lanes] for hr in range(4)]
             base = scalar[...]
@@ -496,7 +519,8 @@
                 send[g * 8 + i] = jnp.where(row8 < cycles, acc, base)
             return inner_carry
 
-        lax.fori_loop(0, groups, shuffle_back, 0)
+        for g in range(groups):
+            shuffle_back(g, 0)
         exchange_start(2 * p + 1)
 
         @pl.when(p == 0)
@@ -527,7 +551,7 @@
                 one_row = slice(4 * half, 4 * half + 1)
 
                 def analyse(t, inner_carry):
-                    at = pl.ds(pl.multiple_of(t * 2 * part, 128), 2 * part)
+                    at = pl.ds(t * 2 * part, 2 * part)
                     out = jnp.dot(both, leg[pair, :, at], preferred_element_type=F32)
                     out = out[0:16] + out[16:32]
                     kept = jnp.where(mask[quad, one_row, at] > 0.5, out[0:8], out[8:16])
@@ -536,7 +560,8 @@
                     partial[quad, 2 * t + 1, mine_rows, 0:part] = value[:, part:2 * part]
                     return inner_carry
 
-                lax.fori_loop(0, n_blk // 2, analyse, 0)
+                for t in range(n_blk // 2):
+                    analyse(t, 0)
                 out = jnp.dot(both, leg[pair, :, degrees:degrees + 128], preferred_element_type=F32)
                 out = out[0:16] + out[16:32]
                 extras[quad, mine_rows, :] = out[8:12] + out[12:16]
@@ -626,18 +651,24 @@
     columns = 16 * n_order
     sheets = -(-(local + 8) // 128)
     half_turn = pixels // 2
-    rows_step = local // 2 if (local // 2) % 16 == 0 else local
+    span = 3 if (degrees // 128) % 3 == 0 else 1
     packed = pl.pallas_call(
-        functools.partial(pack_kernel, degrees, rows_step),
-        grid=(4, local // rows_step),
-        in_specs=[smem, pl.BlockSpec((1, 2, rows_step, degrees), lambda k, b: (k, 0, b, 0)), vmem, vmem, vmem],
-        out_specs=[pl.BlockSpec((1, rows_step, width), lambda k, b: (k, b, 0))] + [vmem] * 9,
+        functools.partial(pack_kernel, degrees, span),
+        in_specs=[smem, hbm, vmem, vmem, vmem],
+        out_specs=[hbm] + [vmem] * 9,
         out_shape=[jax.ShapeDtypeStruct((4, local, width), BF16), jax.ShapeDtypeStruct((8, 128), jnp.int32)]
         + [live_shape, dead_shape] * 3 + [live_shape] * 2,
-        scratch_shapes=[pltpu.VMEM((2, 8, degrees), F32)] * 2,
-        compiler_params=pltpu.CompilerParams(vmem_limit_bytes=VMEM_LIMIT),
+        scratch_shapes=[
+            pltpu.VMEM((4, local, degrees + 128 * span), BF16),
+            pltpu.VMEM((4, local, width), BF16),
+            pltpu.VMEM((2, 2, 8, degrees), F32),
+            pltpu.VMEM((2, 2, 8, degrees), F32),
+            pltpu.SemaphoreType.DMA((4,)),
+            pltpu.SemaphoreType.DMA((4,)),
+        ],
+        compiler_params=pltpu.CompilerParams(vmem_limit_bytes=PACK_VMEM),
         name="pack",
-    )(orders, legendre.reshape(4, 2, local, degrees), right_side, start_guess, prior_inv.reshape(1, degrees))
+    )(orders, legendre, right_side, start_guess, prior_inv.reshape(1, degrees))
     leg, numbers, rhs_live, rhs_dead, x_live, x_dead, prior_live, prior_dead, mask, parity = packed
 
     scratch = [

time: 121 us -> 108 us (0.89)
  Pallas kernels: 120 us -> 107 us
    pallas_call x1, Pallas kernels: 103 us -> 96 us  [per_device(): pl.pallas_call(functools.partial(main_kernel, n_order, n_blk, degrees, cy...]
    pallas_call x1, Pallas kernels: 13.7 us -> 8.47 us  [per_device(): pl.pallas_call(functools.partial(pack_kernel, degrees, span), in_specs=[s...]
where the time goes in v3:
time: 108 us
  Pallas kernels  107 us (99%)
    pallas_call x1, Pallas kernels, per_device(): pl.pallas_call(functools.partial(main_kernel, n_order, n_blk, degrees, cy...  96 us
    pallas_call x1, Pallas kernels, per_device(): pl.pallas_call(functools.partial(pack_kernel, degrees, span), in_specs=[s...  8.47 us
    pallas_call x1, Pallas kernels, per_device(): pl.pallas_call(functools.partial(unpack_kernel, degrees), in_specs=[smem]...  2.89 us

profile of v3, /device:TPU:1, one launch (start us, length us, event | category | flops | bytes accessed | tf_op | source)
XLA Modules:
  0.0 108.0 jit_solution(4151530427729744120)
XLA Ops:
  0.6 8.5 %pack.1 = (bf16[4,192,3200]{2,1,0:T(8,128)(2,1)}, s32[8,128]{1,0:T(8,128)}, f32[2,8,3200]{2,1,0:T(8,128)}, f32[2,8,3072]{2,1,0:T(8,128)}, f32[2,8,3200]{2,1,0:T(...) custom-call(s32[8]{0:T(128)} %orders.3, ...), custom_call_target="tpu_custom_call" | custom-call | tf_op jit(solution)/shard_map/pack/pallas_call | solution.py:655
  9.1 96.0 %steps.1 = (f32[2,8,3200]{2,1,0:T(8,128)}, f32[2,8,3072]{2,1,0:T(8,128)}, f32[2,8,3200]{2,1,0:T(8,128)}, f32[2,8,3072]{2,1,0:T(8,128)}) custom-call(s32[8,128]{1,0:T(8,128)} %get-tuple-element.16.own_orders, bf16[4,192,3200]{2,1,0:T(8,128)(2,1)} %get-tuple-element.17.leg_hbm, f32[2,8,3200]{2,1,0:T(8,128)} %get-tuple-element.18.rhs_live_hbm, ...), custom_call_target="tpu_custom_call" | custom-call | tf_op jit(solution)/shard_map/steps/pallas_call | solution.py:721
  105.1 2.9 %unpack.1 = (f32[2,2,8,3072]{3,2,1,0:T(8,128)}, f32[2,2,8,3072]{3,2,1,0:T(8,128)}) custom-call(s32[8]{0:T(128)} %orders.3, f32[2,8,3200]{2,1,0:T(8,128)} %get-tuple-element.26.x_live, f32[2,8,3072]{2,1,0:T(8,128)} %get-tuple-element.27.x_dead, f32[2,8,3200]{2,1,0:T(8,128)} %get-tuple-element.28.r_live, f32[2,8,3072]{2,1,0:T(8,128)} %get-tuple-element.29.r_dead), custom_call_target="tpu_custom_call" | custom-call | tf_op jit(solution)/shard_map/unpack/pallas_call | solution.py:734

commit v4 on v3

--- a/solution.py
+++ b/solution.py
@@ -171,12 +171,12 @@
 
 
 def main_kernel(n_order, n_blk, degrees, cycles, pixels,
-                own_orders, leg_hbm, rhs_live_hbm, rhs_dead_hbm, x_live, x_dead_hbm, prior_live_hbm, prior_dead_hbm,
-                mask, parity, noise_hbm, flags_hbm,
+                own_orders, leg_hbm, rhs_live_hbm, rhs_dead_hbm, x_live_hbm, x_dead_hbm, prior_live_hbm,
+                prior_dead_hbm, mask_hbm, parity_hbm, noise_hbm, flags_hbm,
                 x_out_live, x_out_dead, r_out_live, r_out_dead,
-                leg, live, dead, rhs_live, rhs_dead, prior_live, prior_dead, noise, flags,
+                leg, leg_turned, live, dead, rhs_live, rhs_dead, prior_live, prior_dead, mask, parity, noise, flags,
                 lhs, modes, turned, back, send, recv, order_recv, scalar,
-                flhs, weight, anal, sign, current, turn, table, sky_kept, pixel_sums,
+                flhs, weight, anal, sign, current, turn, table, table_turned, sky_kept, pixel_sums,
                 partial, extras, shard, rs_recv0, rs_recv1, summed, extra_sum,
                 r1_live, r1_dead, steps,
                 leg_sems, load_sems, order_sems, a2a_send, a2a_recv, rs_send, rs_arrive, ag_send, ag_arrive):
@@ -196,13 +196,9 @@
     def load_copy(at):
         source, target = ((x_dead_hbm, dead.at[0]), (prior_live_hbm, prior_live), (prior_dead_hbm, prior_dead),
                           (noise_hbm, noise), (flags_hbm, flags), (rhs_live_hbm, rhs_live),
-                          (rhs_dead_hbm, rhs_dead))[at]
+                          (rhs_dead_hbm, rhs_dead), (x_live_hbm, live.at[0]), (mask_hbm, mask),
+                          (parity_hbm, parity))[at]
         return pltpu.make_async_copy(source, target, load_sems.at[at])
-
-    for pair in range(4):
-        leg_copy(pair).start()
-    for at in range(7):
-        load_copy(at).start()
 
     side_x = 2
     side_y = n_order // 4
@@ -221,6 +217,12 @@
         pl.semaphore_signal(barrier, inc=1, device_id=(to, mine), device_id_type=MESH)
     for to in partners:
         pl.semaphore_signal(barrier, inc=1, device_id=(me, to), device_id_type=MESH)
+    for at in (7, 8, 9):
+        load_copy(at).start()
+    for pair in range(4):
+        leg_copy(pair).start()
+    for at in range(7):
+        load_copy(at).start()
 
     def wait_bytes(ref, sem):
         pltpu.make_async_copy(ref, ref, sem).wait()
@@ -231,7 +233,8 @@
     turned[...] = jnp.zeros_like(turned)
     scalar[...] = jnp.zeros_like(scalar)
     pixel_sums[...] = jnp.zeros_like(pixel_sums)
-    live[0] = x_live[...]
+    for at in (7, 8, 9):
+        load_copy(at).wait()
 
     pl.semaphore_wait(barrier, n_order - 1 + n_blk - 1)
 
@@ -374,20 +377,26 @@
             for half in range(2):
                 pair = 2 * quad + half
 
+
+                def keep(out, pair=pair, at=4 * half):
+                    out = out[0:32] + out[32:64]
+                    for slot in range(2):
+                        rows = jnp.concatenate([out[16 * slot + at:16 * slot + at + 4],
+                                                out[16 * slot + 8 + at:16 * slot + 8 + at + 4]], axis=0)
+                        if sheets * 128 > local:
+                            rows = jnp.concatenate([rows, jnp.zeros((8, sheets * 128 - local), F32)], axis=1)
+                        for sheet in range(sheets):
+                            modes[sheet, pl.ds(2 * pair + slot, 8, stride=8), :] = (
+                                rows[:, 128 * sheet:128 * sheet + 128])
+
                 @pl.when(p == 0)
                 def _():
                     leg_copy(pair).wait()
-
-                out = lax.dot_general(lhs[quad], leg[pair], NT, preferred_element_type=F32)
-                out = out[0:32] + out[32:64]
-                at = 4 * half
-                for slot in range(2):
-                    rows = jnp.concatenate([out[16 * slot + at:16 * slot + at + 4],
-                                            out[16 * slot + 8 + at:16 * slot + 8 + at + 4]], axis=0)
-                    if sheets * 128 > local:
-                        rows = jnp.concatenate([rows, jnp.zeros((8, sheets * 128 - local), F32)], axis=1)
-                    for sheet in range(sheets):
-                        modes[sheet, pl.ds(2 * pair + slot, 8, stride=8), :] = rows[:, 128 * sheet:128 * sheet + 128]
+                    keep(lax.dot_general(lhs[quad], leg[pair], NT, preferred_element_type=F32))
+
+                @pl.when(p > 0)
+                def _():
+                    keep(jnp.dot(lhs[quad], leg_turned[pair], preferred_element_type=F32))
 
         @pl.when(p > 0)
         def _():
@@ -472,8 +481,17 @@
             sky = sky[0:64] + sky[64:128]
             scaled = sky * weight[:, :, lanes].reshape(64, chunk)
             high, rest = split_bf16(scaled)
-            out = lax.dot_general(jnp.concatenate([high, rest], axis=0), block, NT, preferred_element_type=F32)
-            anal[...] += out[0:64] + out[64:128]
+            both = jnp.concatenate([high, rest], axis=0)
+
+            @pl.when(p == 0)
+            def _():
+                out = lax.dot_general(both, block, NT, preferred_element_type=F32)
+                anal[...] += out[0:64] + out[64:128]
+
+            @pl.when(p > 0)
+            def _():
+                out = jnp.dot(both, table_turned[lanes, :], preferred_element_type=F32)
+                anal[...] += out[0:64] + out[64:128]
 
             @pl.when(p == 1)
             def _():
@@ -527,6 +545,21 @@
         def _():
             for at in (0, 1, 2, 5, 6):
                 load_copy(at).wait()
+
+            def turn_leg(pair, inner_carry):
+                for t in range(width // lane_step):
+                    at = slice(t * lane_step, t * lane_step + lane_step)
+                    leg_turned[pair, at, :] = leg[pair, :, at].T
+                return inner_carry
+
+            lax.fori_loop(0, 4, turn_leg, 0)
+
+            def turn_table(t, inner_carry):
+                at = pl.ds(pl.multiple_of(t * 256, 256), 256)
+                table_turned[at, :] = table[:, at].T
+                return inner_carry
+
+            lax.fori_loop(0, half_turn // 256, turn_table, 0)
 
         for quad in range(2):
             image = prior_dead[quad] * dead[p, quad]
@@ -673,12 +706,15 @@
 
     scratch = [
         pltpu.VMEM((4, local, width), BF16),
+        pltpu.VMEM((4, width, local), BF16),
         pltpu.VMEM((3, 2, 8, width), F32),
         pltpu.VMEM((4, 2, 8, degrees), F32),
         pltpu.VMEM((2, 8, width), F32),
         pltpu.VMEM((2, 8, degrees), F32),
         pltpu.VMEM((2, 8, width), F32),
         pltpu.VMEM((2, 8, degrees), F32),
+        pltpu.VMEM((2, 8, width), F32),
+        pltpu.VMEM((2, 8, width), F32),
         pltpu.VMEM((cycles, 2, pixels), F32),
         pltpu.VMEM((cycles, 2, pixels), jnp.int32),
         pltpu.VMEM((2, 64, width), BF16),
@@ -696,6 +732,7 @@
         pltpu.VMEM((n_order, 2, 8, 128), F32),
         pltpu.VMEM((n_order, 2, 8, 128), F32),
         pltpu.VMEM((columns, half_turn), BF16),
+        pltpu.VMEM((half_turn, columns), BF16),
         pltpu.VMEM((64, half_turn), F32),
         pltpu.VMEM((6, 8, 128), F32),
         pltpu.VMEM((2, n_blk, 8, part + 128), F32),
@@ -709,7 +746,7 @@
         pltpu.VMEM((2, 8, degrees), F32),
         pltpu.VMEM((4, 8, 128), F32),
         pltpu.SemaphoreType.DMA((4,)),
-        pltpu.SemaphoreType.DMA((7,)),
+        pltpu.SemaphoreType.DMA((10,)),
         pltpu.SemaphoreType.DMA((2,)),
         pltpu.SemaphoreType.DMA((6,)),
         pltpu.SemaphoreType.DMA((6,)),
@@ -720,7 +757,7 @@
     ]
     results = pl.pallas_call(
         functools.partial(main_kernel, n_order, n_blk, degrees, cycles, pixels),
-        in_specs=[vmem, hbm, hbm, hbm, vmem, hbm, hbm, hbm, vmem, vmem, hbm, hbm],
+        in_specs=[vmem] + [hbm] * 11,
         out_specs=[vmem] * 4,
         out_shape=[live_shape, dead_shape, live_shape, dead_shape],
         scratch_shapes=scratch,

time: 108 us -> 105 us (0.972)
  Pallas kernels: 107 us -> 104 us
    pallas_call x1, Pallas kernels: 96 us -> 93.1 us  [per_device(): pl.pallas_call(functools.partial(main_kernel, n_order, n_blk, degrees, cy...]
where the time goes in v4:
time: 105 us
  Pallas kernels  104 us (99%)
    pallas_call x1, Pallas kernels, per_device(): pl.pallas_call(functools.partial(main_kernel, n_order, n_blk, degrees, cy...  93.1 us
    pallas_call x1, Pallas kernels, per_device(): pl.pallas_call(functools.partial(pack_kernel, degrees, span), in_specs=[s...  8.47 us
    pallas_call x1, Pallas kernels, per_device(): pl.pallas_call(functools.partial(unpack_kernel, degrees), in_specs=[smem]...  2.89 us

profile of v4, /device:TPU:1, one launch (start us, length us, event | category | flops | bytes accessed | tf_op | source)
XLA Modules:
  0.0 105.1 jit_solution(17378679098185104925)
XLA Ops:
  0.6 8.5 %pack.1 = (bf16[4,192,3200]{2,1,0:T(8,128)(2,1)}, s32[8,128]{1,0:T(8,128)}, f32[2,8,3200]{2,1,0:T(8,128)}, f32[2,8,3072]{2,1,0:T(8,128)}, f32[2,8,3200]{2,1,0:T(...) custom-call(s32[8]{0:T(128)} %orders.3, ...), custom_call_target="tpu_custom_call" | custom-call | tf_op jit(solution)/shard_map/pack/pallas_call | solution.py:688
  9.1 93.1 %steps.1 = (f32[2,8,3200]{2,1,0:T(8,128)}, f32[2,8,3072]{2,1,0:T(8,128)}, f32[2,8,3200]{2,1,0:T(8,128)}, f32[2,8,3072]{2,1,0:T(8,128)}) custom-call(s32[8,128]{1,0:T(8,128)} %get-tuple-element.16.own_orders, bf16[4,192,3200]{2,1,0:T(8,128)(2,1)} %get-tuple-element.17.leg_hbm, f32[2,8,3200]{2,1,0:T(8,128)} %get-tuple-element.18.rhs_live_hbm, ...), custom_call_target="tpu_custom_call" | custom-call | tf_op jit(solution)/shard_map/steps/pallas_call | solution.py:758
  102.2 2.9 %unpack.1 = (f32[2,2,8,3072]{3,2,1,0:T(8,128)}, f32[2,2,8,3072]{3,2,1,0:T(8,128)}) custom-call(s32[8]{0:T(128)} %orders.3, f32[2,8,3200]{2,1,0:T(8,128)} %get-tuple-element.26.x_live, f32[2,8,3072]{2,1,0:T(8,128)} %get-tuple-element.27.x_dead, f32[2,8,3200]{2,1,0:T(8,128)} %get-tuple-element.28.r_live, f32[2,8,3072]{2,1,0:T(8,128)} %get-tuple-element.29.r_dead), custom_call_target="tpu_custom_call" | custom-call | tf_op jit(solution)/shard_map/unpack/pallas_call | solution.py:771

commit v5 on v4

--- a/solution.py
+++ b/solution.py
@@ -11,7 +11,6 @@
 F32 = jnp.float32
 BF16 = jnp.bfloat16
 VMEM_LIMIT = 56 * 1024 * 1024
-PACK_VMEM = 56 * 1024 * 1024
 NT = (((1,), (1,)), ((), ()))
 
 
@@ -33,103 +32,16 @@
         before = now
 
 
-def pack_kernel(degrees, span, orders, leg_hbm, rhs, guess, prior,
-                leg_out, numbers, rhs_live, rhs_dead, x_live, x_dead, prior_live, prior_dead,
-                mask, parity, stage, packed, rows_a, rows_b, in_sems, out_sems):
-    tiles = degrees // 128
-    blocks = tiles // span
-    local = packed.shape[1]
-    lane16 = iota((16, 128), 1)
-    lane8 = iota((8, 128), 1)
-    row8 = iota((8, 128), 0)
-    upper = row8 < 4
-
-    for pair in range(4):
-        own_blocks = orders[2 * pair] // (128 * span)
-        for j in range(blocks + 1):
-            second = j <= own_blocks
-            slot = 2 * pair + jnp.where(second, 1, 0)
-            column = jnp.where(second, blocks - 1 - own_blocks + j, j - 1) * (128 * span)
-            lanes = pl.ds(pl.multiple_of(column, 128), 128 * span)
-            pltpu.make_async_copy(leg_hbm.at[slot, :, lanes],
-                                  stage.at[pair, :, pl.ds(j * 128 * span, 128 * span)], in_sems.at[pair]).start()
-
-    tile = jnp.zeros((8, 128), jnp.int32)
-    for m in range(8):
-        tile = jnp.where(row8 == m, orders[m], tile)
-    numbers[...] = tile
-    tail = slice(degrees, degrees + 128)
-    sources = [(rhs, rhs_live, rhs_dead), (guess, x_live, x_dead)]
-    for quad in range(2):
-        low, high = orders[4 * quad], orders[4 * quad + 2]
-        shifts = jnp.where(upper, low, high)
-        number_b = jnp.where(upper, orders[4 * quad + 1], orders[4 * quad + 3])
-        for at, (source, live, dead) in enumerate(sources):
-            for half in range(2):
-                slot = 4 * quad + 2 * half
-                for r in range(2):
-                    for c in range(2):
-                        row = half * 4 + r * 2 + c
-                        rows_a[quad, at, row:row + 1, :] = source[r, c, slot:slot + 1, :]
-                        rows_b[quad, at, row:row + 1, :] = source[r, c, slot + 1:slot + 2, :]
-
-        def both(load):
-            for one, two in zip(rolled_tiles(load, low, tiles, lane8), rolled_tiles(load, high, tiles, lane8)):
-                yield jnp.where(upper, one, two)
-
-        for at, (source, live, dead) in enumerate(sources):
-            for t, rolled in enumerate(both(lambda lanes: rows_b[quad, at, :, lanes])):
-                lanes = slice(t * 128, t * 128 + 128)
-                own = lane8 + t * 128 >= shifts
-                first = rows_a[quad, at, :, lanes]
-                idle = jnp.where(own, rolled, first)
-                if t == tiles - 1:
-                    idle = jnp.where(lane8 == 127, 0.0, idle)
-                live[quad, :, lanes] = jnp.where(own, first, rolled)
-                dead[quad, :, lanes] = idle
-            live[quad, :, tail] = jnp.where(lane8 == 0, pltpu.roll(rolled, 1, 1), 0.0)
-        for t, rolled in enumerate(both(lambda lanes: jnp.broadcast_to(prior[:, lanes], (8, 128)))):
-            lanes = slice(t * 128, t * 128 + 128)
-            place = lane8 + t * 128
-            own = place >= shifts
-            first = jnp.broadcast_to(prior[:, lanes], (8, 128))
-            prior_live[quad, :, lanes] = jnp.where(own, first, rolled)
-            prior_dead[quad, :, lanes] = jnp.where(own, rolled, first)
-            total = jnp.where(own, place + shifts, place - shifts + degrees + number_b)
-            parity[quad, :, lanes] = (1 - 2 * (total & 1)).astype(F32)
-            mask[quad, :, lanes] = own.astype(F32)
-        prior_live[quad, :, tail] = jnp.where(lane8 == 0, pltpu.roll(rolled, 1, 1), 0.0)
-        parity[quad, :, tail] = jnp.ones((8, 128), F32)
-        mask[quad, :, tail] = jnp.zeros((8, 128), F32)
-
-    for pair in range(4):
-        shift = orders[2 * pair]
-        within = lax.rem(shift, 128)
-        back = span - 1 - lax.rem(shift // 128, span)
-        pltpu.make_async_copy(stage.at[pair], stage.at[pair], in_sems.at[pair]).wait()
-
-        def rows_of(step, carry):
-            rows = pl.ds(pl.multiple_of(step * 16, 16), 16)
-
-            def moved(t):
-                lanes = pl.ds(pl.multiple_of((t + back) * 128, 128), 128)
-                return pltpu.roll(stage[pair, rows, lanes], within, 1)
-
-            before = moved(0)
-            extra = jnp.where(lane16 == 0, pltpu.roll(before, 1, 1), jnp.zeros_like(before))
-            packed[pair, rows, degrees:degrees + 128] = extra
-            for t in range(tiles):
-                now = moved(t + 1)
-                rolled = jnp.where(lane16 >= within, now, before)
-                first = stage[pair, rows, (t + span) * 128:(t + span) * 128 + 128]
-                packed[pair, rows, t * 128:t * 128 + 128] = jnp.where(lane16 + t * 128 >= shift, first, rolled)
-                before = now
-            return carry
-
-        lax.fori_loop(0, local // 16, rows_of, 0, unroll=4 if local % 64 == 0 else 1)
-        pltpu.make_async_copy(packed.at[pair], leg_out.at[pair], out_sems.at[pair]).start()
-    for pair in range(4):
-        pltpu.make_async_copy(packed.at[pair], leg_out.at[pair], out_sems.at[pair]).wait()
+def rotate_tiles(tiles, whole):
+    count = len(tiles)
+    for bit in range((count - 1).bit_length()):
+        moved = (whole & (1 << bit)) != 0
+        tiles = [jnp.where(moved, tiles[(t - (1 << bit)) % count], tiles[t]) for t in range(count)]
+    return tiles
+
+
+def lane_shift(value, within):
+    return pltpu.roll(value, within, 1)
 
 
 def unpack_kernel(degrees, orders, x_live, x_dead, r_live, r_dead, x_out, r_out, rows_a, rows_b):
@@ -171,9 +83,9 @@
 
 
 def main_kernel(n_order, n_blk, degrees, cycles, pixels,
-                own_orders, leg_hbm, rhs_live_hbm, rhs_dead_hbm, x_live_hbm, x_dead_hbm, prior_live_hbm,
-                prior_dead_hbm, mask_hbm, parity_hbm, noise_hbm, flags_hbm,
+                orders, leg_hbm, guess_hbm, rhs_hbm, prior, noise_hbm, flags_hbm,
                 x_out_live, x_out_dead, r_out_live, r_out_dead,
+                raw0, raw1, raw2, raw3, own_orders, guess, rhs, rows_a, rows_b,
                 leg, leg_turned, live, dead, rhs_live, rhs_dead, prior_live, prior_dead, mask, parity, noise, flags,
                 lhs, modes, turned, back, send, recv, order_recv, scalar,
                 flhs, weight, anal, sign, current, turn, table, table_turned, sky_kept, pixel_sums,
@@ -190,15 +102,18 @@
     part = degrees // n_blk
     sheets = modes.shape[0]
 
+    raws = (raw0, raw1, raw2, raw3)
+
     def leg_copy(pair):
-        return pltpu.make_async_copy(leg_hbm.at[pair], leg.at[pair], leg_sems.at[pair])
+        return pltpu.make_async_copy(leg_hbm.at[pl.ds(2 * pair, 2)], raws[pair], leg_sems.at[pair])
 
     def load_copy(at):
-        source, target = ((x_dead_hbm, dead.at[0]), (prior_live_hbm, prior_live), (prior_dead_hbm, prior_dead),
-                          (noise_hbm, noise), (flags_hbm, flags), (rhs_live_hbm, rhs_live),
-                          (rhs_dead_hbm, rhs_dead), (x_live_hbm, live.at[0]), (mask_hbm, mask),
-                          (parity_hbm, parity))[at]
+        source, target = ((guess_hbm, guess), (rhs_hbm, rhs), (noise_hbm, noise), (flags_hbm, flags))[at]
         return pltpu.make_async_copy(source, target, load_sems.at[at])
+
+    load_copy(0).start()
+    for pair in range(4):
+        leg_copy(pair).start()
 
     side_x = 2
     side_y = n_order // 4
@@ -217,11 +132,7 @@
         pl.semaphore_signal(barrier, inc=1, device_id=(to, mine), device_id_type=MESH)
     for to in partners:
         pl.semaphore_signal(barrier, inc=1, device_id=(me, to), device_id_type=MESH)
-    for at in (7, 8, 9):
-        load_copy(at).start()
-    for pair in range(4):
-        leg_copy(pair).start()
-    for at in range(7):
+    for at in (1, 2, 3):
         load_copy(at).start()
 
     def wait_bytes(ref, sem):
@@ -233,8 +144,76 @@
     turned[...] = jnp.zeros_like(turned)
     scalar[...] = jnp.zeros_like(scalar)
     pixel_sums[...] = jnp.zeros_like(pixel_sums)
-    for at in (7, 8, 9):
-        load_copy(at).wait()
+    upper8 = row8 < 4
+    lane16 = iota((16, 128), 1)
+    zero16 = iota((16, 128), 0) * 0
+
+    def shift_rows(quad):
+        return jnp.where(upper8, orders[4 * quad], orders[4 * quad + 2])
+
+    def rolled_rows(values, quad):
+        shifts = shift_rows(quad)
+        whole, within = shifts // 128, shifts % 128
+        low, high = orders[4 * quad] % 128, orders[4 * quad + 2] % 128
+        moved = [jnp.where(upper8, lane_shift(value, low), lane_shift(value, high))
+                 for value in rotate_tiles(values, whole)]
+        return [jnp.where(lane8 >= within, moved[t], moved[t - 1]) for t in range(tiles)]
+
+    def split_vector(source, live_out, dead_out):
+        for quad in range(2):
+            for half in range(2):
+                slot = 4 * quad + 2 * half
+                for r in range(2):
+                    for c in range(2):
+                        row = half * 4 + r * 2 + c
+                        rows_a[quad, row:row + 1, :] = source[r, c, slot:slot + 1, :]
+                        rows_b[quad, row:row + 1, :] = source[r, c, slot + 1:slot + 2, :]
+            shifts = shift_rows(quad)
+            rolled = rolled_rows([rows_b[quad, :, t * 128:t * 128 + 128] for t in range(tiles)], quad)
+            for t in range(tiles):
+                lanes = slice(t * 128, t * 128 + 128)
+                own = lane8 + t * 128 >= shifts
+                first = rows_a[quad, :, lanes]
+                idle = jnp.where(own, rolled[t], first)
+                if t == tiles - 1:
+                    idle = jnp.where(lane8 == 127, 0.0, idle)
+                live_out[quad, :, lanes] = jnp.where(own, first, rolled[t])
+                dead_out[quad, :, lanes] = idle
+            live_out[quad, :, degrees:degrees + 128] = jnp.where(lane8 == 0, pltpu.roll(rolled[-1], 1, 1), 0.0)
+
+    def split_prior():
+        for quad in range(2):
+            shifts = shift_rows(quad)
+            firsts = [jnp.broadcast_to(prior[:, t * 128:t * 128 + 128], (8, 128)) for t in range(tiles)]
+            rolled = rolled_rows(firsts, quad)
+            for t in range(tiles):
+                lanes = slice(t * 128, t * 128 + 128)
+                own = lane8 + t * 128 >= shifts
+                prior_live[quad, :, lanes] = jnp.where(own, firsts[t], rolled[t])
+                prior_dead[quad, :, lanes] = jnp.where(own, rolled[t], firsts[t])
+            prior_live[quad, :, degrees:degrees + 128] = jnp.where(lane8 == 0, pltpu.roll(rolled[-1], 1, 1), 0.0)
+
+    def fill_masks():
+        for quad in range(2):
+            shifts = shift_rows(quad)
+            number_b = jnp.where(upper8, orders[4 * quad + 1], orders[4 * quad + 3])
+            for t in range(tiles):
+                lanes = slice(t * 128, t * 128 + 128)
+                place = lane8 + t * 128
+                own = place >= shifts
+                total = jnp.where(own, place + shifts, place - shifts + degrees + number_b)
+                parity[quad, :, lanes] = (1 - 2 * (total & 1)).astype(F32)
+                mask[quad, :, lanes] = own.astype(F32)
+            parity[quad, :, degrees:degrees + 128] = jnp.ones((8, 128), F32)
+            mask[quad, :, degrees:degrees + 128] = jnp.zeros((8, 128), F32)
+
+    tile = jnp.zeros((8, 128), jnp.int32)
+    for m in range(8):
+        tile = jnp.where(row8 == m, orders[m], tile)
+    own_orders[...] = tile
+    fill_masks()
+    load_copy(0).wait()
+    split_vector(guess, live.at[0], dead.at[0])
 
     pl.semaphore_wait(barrier, n_order - 1 + n_blk - 1)
 
@@ -244,6 +223,27 @@
             send_sem=order_sems.at[0], recv_sem=order_sems.at[1],
             device_id=(to, mine), device_id_type=MESH).start()
     order_recv[me] = own_orders[...]
+
+    for pair in range(4):
+        leg_copy(pair).wait()
+        raw = raws[pair]
+        shift = orders[2 * pair]
+        within = shift % 128
+        whole = zero16 + shift // 128
+
+        def pack_rows(step, carry):
+            rows = pl.ds(pl.multiple_of(step * 16, 16), 16)
+            moved = rotate_tiles([raw[1, rows, t * 128:t * 128 + 128] for t in range(tiles)], whole)
+            moved = [lane_shift(value, within) for value in moved]
+            for t in range(tiles):
+                rolled = jnp.where(lane16 >= within, moved[t], moved[t - 1])
+                first = raw[0, rows, t * 128:t * 128 + 128]
+                leg[pair, rows, t * 128:t * 128 + 128] = jnp.where(lane16 + t * 128 >= shift, first, rolled)
+            extra = jnp.where(lane16 == 0, pltpu.roll(rolled, 1, 1), jnp.zeros_like(rolled))
+            leg[pair, rows, degrees:degrees + 128] = extra
+            return carry
+
+        lax.fori_loop(0, local // 16, pack_rows, 0, unroll=4 if local % 64 == 0 else 1)
 
     def exchange_start(step):
         for to in peers:
@@ -391,7 +391,6 @@
 
                 @pl.when(p == 0)
                 def _():
-                    leg_copy(pair).wait()
                     keep(lax.dot_general(lhs[quad], leg[pair], NT, preferred_element_type=F32))
 
                 @pl.when(p > 0)
@@ -422,9 +421,10 @@
         @pl.when(p == 0)
         def _():
             build_table()
+            load_copy(2).wait()
             load_copy(3).wait()
-            load_copy(4).wait()
             build_weight()
+            split_prior()
 
         exchange_wait(2 * p)
 
@@ -543,8 +543,8 @@
 
         @pl.when(p == 0)
         def _():
-            for at in (0, 1, 2, 5, 6):
-                load_copy(at).wait()
+            load_copy(1).wait()
+            split_vector(rhs, rhs_live, rhs_dead)
 
             def turn_leg(pair, inner_carry):
                 for t in range(width // lane_step):
@@ -684,27 +684,12 @@
     columns = 16 * n_order
     sheets = -(-(local + 8) // 128)
     half_turn = pixels // 2
-    span = 3 if (degrees // 128) % 3 == 0 else 1
-    packed = pl.pallas_call(
-        functools.partial(pack_kernel, degrees, span),
-        in_specs=[smem, hbm, vmem, vmem, vmem],
-        out_specs=[hbm] + [vmem] * 9,
-        out_shape=[jax.ShapeDtypeStruct((4, local, width), BF16), jax.ShapeDtypeStruct((8, 128), jnp.int32)]
-        + [live_shape, dead_shape] * 3 + [live_shape] * 2,
-        scratch_shapes=[
-            pltpu.VMEM((4, local, degrees + 128 * span), BF16),
-            pltpu.VMEM((4, local, width), BF16),
-            pltpu.VMEM((2, 2, 8, degrees), F32),
-            pltpu.VMEM((2, 2, 8, degrees), F32),
-            pltpu.SemaphoreType.DMA((4,)),
-            pltpu.SemaphoreType.DMA((4,)),
-        ],
-        compiler_params=pltpu.CompilerParams(vmem_limit_bytes=PACK_VMEM),
-        name="pack",
-    )(orders, legendre, right_side, start_guess, prior_inv.reshape(1, degrees))
-    leg, numbers, rhs_live, rhs_dead, x_live, x_dead, prior_live, prior_dead, mask, parity = packed
-
-    scratch = [
+    scratch = [pltpu.VMEM((2, local, degrees), BF16)] * 4 + [
+        pltpu.VMEM((8, 128), jnp.int32),
+        pltpu.VMEM(right_side.shape, F32),
+        pltpu.VMEM(right_side.shape, F32),
+        pltpu.VMEM((2, 8, degrees), F32),
+        pltpu.VMEM((2, 8, degrees), F32),
         pltpu.VMEM((4, local, width), BF16),
         pltpu.VMEM((4, width, local), BF16),
         pltpu.VMEM((3, 2, 8, width), F32),
@@ -746,7 +731,7 @@
         pltpu.VMEM((2, 8, degrees), F32),
         pltpu.VMEM((4, 8, 128), F32),
         pltpu.SemaphoreType.DMA((4,)),
-        pltpu.SemaphoreType.DMA((10,)),
+        pltpu.SemaphoreType.DMA((4,)),
         pltpu.SemaphoreType.DMA((2,)),
         pltpu.SemaphoreType.DMA((6,)),
         pltpu.SemaphoreType.DMA((6,)),
@@ -757,14 +742,14 @@
     ]
     results = pl.pallas_call(
         functools.partial(main_kernel, n_order, n_blk, degrees, cycles, pixels),
-        in_specs=[vmem] + [hbm] * 11,
+        in_specs=[smem, hbm, hbm, hbm, vmem, hbm, hbm],
         out_specs=[vmem] * 4,
         out_shape=[live_shape, dead_shape, live_shape, dead_shape],
         scratch_shapes=scratch,
         compiler_params=pltpu.CompilerParams(
             collective_id=0, has_side_effects=True, vmem_limit_bytes=VMEM_LIMIT),
         name="steps",
-    )(numbers, leg, rhs_live, rhs_dead, x_live, x_dead, prior_live, prior_dead, mask, parity,
+    )(orders, legendre, start_guess, right_side, prior_inv.reshape(1, degrees),
       noise_inv.transpose(1, 0, 2), pixel_flags.transpose(1, 0, 2))
 
     full = jax.ShapeDtypeStruct(right_side.shape, F32)

time: 105 us -> 99.8 us (0.950)
  Pallas kernels: 104 us -> 98.5 us
    pallas_call x1 -> x0, Pallas kernels: 8.47 us -> none  [per_device(): pl.pallas_call(functools.partial(pack_kernel, degrees, span), in_specs=[s...]
    pallas_call x1, Pallas kernels: 93.1 us -> 95.6 us  [per_device(): pl.pallas_call(functools.partial(main_kernel, n_order, n_blk, degrees, cy...]
where the time goes in v5:
time: 99.8 us; the launch traced here: 99.1 us
  Pallas kernels  98.5 us (99%)
    pallas_call x1, Pallas kernels, per_device(): pl.pallas_call(functools.partial(main_kernel, n_order, n_blk, degrees, cy...  95.6 us
    pallas_call x1, Pallas kernels, per_device(): pl.pallas_call(functools.partial(unpack_kernel, degrees), in_specs=[smem]...  2.89 us

profile of v5, /device:TPU:1, one launch (start us, length us, event | category | flops | bytes accessed | tf_op | source)
XLA Modules:
  0.0 99.1 jit_solution(13793383092316890150)
XLA Ops:
  0.6 95.6 %steps.1 = (f32[2,8,3200]{2,1,0:T(8,128)}, f32[2,8,3072]{2,1,0:T(8,128)}, f32[2,8,3200]{2,1,0:T(8,128)}, f32[2,8,3072]{2,1,0:T(8,128)}) custom-call(s32[8]{0:T(128)} %orders.3, bf16[8,192,3072]{2,1,0:T(8,128)(2,1)} %leg_hbm.1, f32[2,2,8,3072]{3,2,1,0:T(8,128)} %guess_hbm.1, f32[2,2,8,3072]{3,2,1,0:T(8,128)} %rhs_hbm.1, f32[1,3072]{1,0:T(1,128)} %bitcast.5, ...), custom_call_target="tpu_custom_call" | custom-call | tf_op jit(solution)/shard_map/steps/pallas_call | solution.py:743
  96.2 2.9 %unpack.1 = (f32[2,2,8,3072]{3,2,1,0:T(8,128)}, f32[2,2,8,3072]{3,2,1,0:T(8,128)}) custom-call(s32[8]{0:T(128)} %orders.3, f32[2,8,3200]{2,1,0:T(8,128)} %get-tuple-element.6.x_live, f32[2,8,3072]{2,1,0:T(8,128)} %get-tuple-element.7.x_dead, f32[2,8,3200]{2,1,0:T(8,128)} %get-tuple-element.8.r_live, f32[2,8,3072]{2,1,0:T(8,128)} %get-tuple-element.9.r_dead), custom_call_target="tpu_custom_call" | custom-call | tf_op jit(solution)/shard_map/unpack/pallas_call | solution.py:756

commit v6 on v5

--- a/solution.py
+++ b/solution.py
@@ -42,6 +42,30 @@
 
 def lane_shift(value, within):
     return pltpu.roll(value, within, 1)
+
+
+def split_rows(value, first, flip):
+    high = value.astype(BF16).astype(F32)
+    pieces = []
+    for piece in (high, value - high):
+        for keep in (first, 1.0 - first):
+            kept = piece * keep
+            pieces.append(kept)
+            pieces.append(kept * flip)
+    return jnp.concatenate(pieces, axis=0).astype(BF16)
+
+
+def place_modes(modes, out, pair, local):
+    sheets = modes.shape[0]
+    at = 4 * (pair % 2)
+    out = out[0:32] + out[32:64]
+    for slot in range(2):
+        rows = jnp.concatenate([out[16 * slot + at:16 * slot + at + 4],
+                                out[16 * slot + 8 + at:16 * slot + 8 + at + 4]], axis=0)
+        if sheets * 128 > local:
+            rows = jnp.concatenate([rows, jnp.zeros((8, sheets * 128 - local), F32)], axis=1)
+        for sheet in range(sheets):
+            modes[sheet, pl.ds(2 * pair + slot, 8, stride=8), :] = rows[:, 128 * sheet:128 * sheet + 128]
 
 
 def unpack_kernel(degrees, orders, x_live, x_dead, r_live, r_dead, x_out, r_out, rows_a, rows_b):
@@ -111,7 +135,8 @@
         source, target = ((guess_hbm, guess), (rhs_hbm, rhs), (noise_hbm, noise), (flags_hbm, flags))[at]
         return pltpu.make_async_copy(source, target, load_sems.at[at])
 
-    load_copy(0).start()
+    for at in (0, 2, 3):
+        load_copy(at).start()
     for pair in range(4):
         leg_copy(pair).start()
 
@@ -132,8 +157,7 @@
         pl.semaphore_signal(barrier, inc=1, device_id=(to, mine), device_id_type=MESH)
     for to in partners:
         pl.semaphore_signal(barrier, inc=1, device_id=(me, to), device_id_type=MESH)
-    for at in (1, 2, 3):
-        load_copy(at).start()
+    load_copy(1).start()
 
     def wait_bytes(ref, sem):
         pltpu.make_async_copy(ref, ref, sem).wait()
@@ -211,9 +235,38 @@
     for m in range(8):
         tile = jnp.where(row8 == m, orders[m], tile)
     own_orders[...] = tile
+    def build_weight():
+        weight[...] = jnp.zeros_like(weight)
+        for j in range(cycles):
+            value = noise[j] * flags[j].astype(F32)
+            for h in range(2):
+                for image in range(2):
+                    row = value[h:h + 1, image * half_turn:(image + 1) * half_turn]
+                    for r in range(2):
+                        weight[image * 4 + h * 2 + r, j:j + 1, :] = row
+
     fill_masks()
     load_copy(0).wait()
     split_vector(guess, live.at[0], dead.at[0])
+    split_prior()
+    load_copy(2).wait()
+    load_copy(3).wait()
+    build_weight()
+
+    width = degrees + 128
+    lane_step = 128 * max(n for n in (5, 3, 1) if (tiles + 1) % n == 0)
+
+    def build_rows(p, quad):
+        for t in range(width // lane_step):
+            at = pl.ds(t * lane_step, lane_step)
+            lhs[quad, :, at] = split_rows(live[p, quad, :, at], mask[quad, :, at], parity[quad, :, at])
+
+    def turn_modes():
+        for sheet in range(sheets):
+            turned[128 * sheet:128 * sheet + 128, :] = modes[sheet].T
+
+    for quad in range(2):
+        build_rows(0, quad)
 
     pl.semaphore_wait(barrier, n_order - 1 + n_blk - 1)
 
@@ -244,6 +297,9 @@
             return carry
 
         lax.fori_loop(0, local // 16, pack_rows, 0, unroll=4 if local % 64 == 0 else 1)
+        place_modes(modes, lax.dot_general(lhs[pair // 2], leg[pair], NT, preferred_element_type=F32), pair, local)
+
+    turn_modes()
 
     def exchange_start(step):
         for to in peers:
@@ -256,16 +312,6 @@
     def exchange_wait(step):
         wait_bytes(recv.at[step, pl.ds(0, n_order - 1)], a2a_recv.at[step])
         wait_bytes(send.at[pl.ds(0, n_order - 1)], a2a_send.at[step])
-
-    def build_weight():
-        weight[...] = jnp.zeros_like(weight)
-        for j in range(cycles):
-            value = noise[j] * flags[j].astype(F32)
-            for h in range(2):
-                for image in range(2):
-                    row = value[h:h + 1, image * half_turn:(image + 1) * half_turn]
-                    for r in range(2):
-                        weight[image * 4 + h * 2 + r, j:j + 1, :] = row
 
     def build_table():
         wait_bytes(order_recv.at[pl.ds(0, n_order - 1)], order_sems.at[1])
@@ -289,23 +335,20 @@
         sign_rows = jnp.concatenate([odd, odd], axis=1).reshape(columns, 128)
         sign[...] = sign_rows.T[0:8]
 
-        def block(q, carry):
-            lanes = pl.ds(pl.multiple_of(q * 128, 128), 128)
-
-            def some(piece, inner):
+        def some(piece, inner):
+            held = []
+            for k in range(8):
+                s = piece * 8 + k
+                held.append((current[s, 0], current[s, 1], turn[s, 0], turn[s, 1]))
+            for q in range(half_turn // 128):
                 for k in range(8):
-                    s = piece * 8 + k
-                    cosine, sine = current[s, 0], current[s, 1]
-                    rows = pl.ds(pl.multiple_of(s * 16, 16), 16)
-                    table[rows, lanes] = jnp.concatenate([cosine, sine], axis=0).astype(BF16)
-                    turn_c, turn_s = turn[s, 0], turn[s, 1]
-                    current[s, 0] = cosine * turn_c + sine * turn_s
-                    current[s, 1] = sine * turn_c - cosine * turn_s
-                return inner
-
-            return lax.fori_loop(0, n_order // 8, some, carry)
-
-        lax.fori_loop(0, half_turn // 128, block, 0)
+                    cosine, sine, turn_c, turn_s = held[k]
+                    rows = pl.ds(pl.multiple_of((piece * 8 + k) * 16, 16), 16)
+                    table[rows, q * 128:q * 128 + 128] = jnp.concatenate([cosine, sine], axis=0).astype(BF16)
+                    held[k] = (cosine * turn_c + sine * turn_s, sine * turn_c - cosine * turn_s, turn_c, turn_s)
+            return inner
+
+        lax.fori_loop(0, n_order // 8, some, 0)
 
     group8 = lane8 // 16
     item8 = lane8 // 8
@@ -340,13 +383,11 @@
     def pair_at(total, row, at):
         return [scalar_at(total, row, at), scalar_at(total, row, at + 1)]
 
-    lane_step = 128 * max(n for n in (5, 3, 1) if (tiles + 1) % n == 0)
-    width = degrees + 128
 
     def application(p, carry):
-        for quad in range(2):
-            @pl.when(p > 0)
-            def _():
+        @pl.when(p > 0)
+        def _():
+            for quad in range(2):
                 wait_bytes(rs_recv0.at[p - 1, pl.ds(0, n_blk - 1)], ag_arrive.at[p - 1, quad])
                 main = pl.ds(0, degrees)
                 image = prior_live[quad, :, main] * live[p - 1, quad, :, main] + summed[p - 1, quad]
@@ -354,56 +395,13 @@
                 tail = pl.ds(degrees, 128)
                 image = prior_live[quad, :, tail] * live[p - 1, quad, :, tail] + extra_sum[quad]
                 live[p, quad, :, tail] = jnp.where(p == 1, rhs_live[quad, :, tail] - image, image)
-
-            def build(t, inner_carry):
-                at = pl.ds(t * lane_step, lane_step)
-                value = live[p, quad, :, at]
-                first = mask[quad, :, at]
-                second = 1.0 - first
-                flip = parity[quad, :, at]
-                high = value.astype(BF16).astype(F32)
-                rest = value - high
-                pieces = []
-                for piece in (high, rest):
-                    for keep in (first, second):
-                        kept = piece * keep
-                        pieces.append(kept)
-                        pieces.append(kept * flip)
-                lhs[quad, :, at] = jnp.concatenate(pieces, axis=0).astype(BF16)
-                return inner_carry
-
-            for t in range(width // lane_step):
-                build(t, 0)
-            for half in range(2):
-                pair = 2 * quad + half
-
-
-                def keep(out, pair=pair, at=4 * half):
-                    out = out[0:32] + out[32:64]
-                    for slot in range(2):
-                        rows = jnp.concatenate([out[16 * slot + at:16 * slot + at + 4],
-                                                out[16 * slot + 8 + at:16 * slot + 8 + at + 4]], axis=0)
-                        if sheets * 128 > local:
-                            rows = jnp.concatenate([rows, jnp.zeros((8, sheets * 128 - local), F32)], axis=1)
-                        for sheet in range(sheets):
-                            modes[sheet, pl.ds(2 * pair + slot, 8, stride=8), :] = (
-                                rows[:, 128 * sheet:128 * sheet + 128])
-
-                @pl.when(p == 0)
-                def _():
-                    keep(lax.dot_general(lhs[quad], leg[pair], NT, preferred_element_type=F32))
-
-                @pl.when(p > 0)
-                def _():
-                    keep(jnp.dot(lhs[quad], leg_turned[pair], preferred_element_type=F32))
-
-        @pl.when(p > 0)
-        def _():
+                build_rows(p, quad)
+                for half in range(2):
+                    pair = 2 * quad + half
+                    place_modes(modes, jnp.dot(lhs[quad], leg_turned[pair], preferred_element_type=F32), pair, local)
             for quad in range(2):
                 wait_bytes(rs_recv0.at[p - 1, pl.ds(0, n_blk - 1)], ag_send.at[p - 1, quad])
-
-        for sheet in range(sheets):
-            turned[128 * sheet:128 * sheet + 128, :] = modes[sheet].T
+            turn_modes()
 
         @pl.when(p == 2)
         def _():
@@ -421,10 +419,13 @@
         @pl.when(p == 0)
         def _():
             build_table()
-            load_copy(2).wait()
-            load_copy(3).wait()
-            build_weight()
-            split_prior()
+
+            def turn_table(t, inner_carry):
+                at = pl.ds(pl.multiple_of(t * 256, 256), 256)
+                table_turned[at, :] = table[:, at].T
+                return inner_carry
+
+            lax.fori_loop(0, half_turn // 256, turn_table, 0)
 
         exchange_wait(2 * p)
 
@@ -472,7 +473,7 @@
             shuffle(g, 0)
 
         anal[...] = jnp.zeros_like(anal)
-        chunk = min(1536, half_turn)
+        chunk = min(3072, half_turn)
 
         def fourier(t, inner_carry):
             lanes = pl.ds(pl.multiple_of(t * chunk, 128), chunk)
@@ -483,15 +484,8 @@
             high, rest = split_bf16(scaled)
             both = jnp.concatenate([high, rest], axis=0)
 
-            @pl.when(p == 0)
-            def _():
-                out = lax.dot_general(both, block, NT, preferred_element_type=F32)
-                anal[...] += out[0:64] + out[64:128]
-
-            @pl.when(p > 0)
-            def _():
-                out = jnp.dot(both, table_turned[lanes, :], preferred_element_type=F32)
-                anal[...] += out[0:64] + out[64:128]
+            out = jnp.dot(both, table_turned[lanes, :], preferred_element_type=F32)
+            anal[...] += out[0:64] + out[64:128]
 
             @pl.when(p == 1)
             def _():
@@ -553,13 +547,6 @@
                 return inner_carry
 
             lax.fori_loop(0, 4, turn_leg, 0)
-
-            def turn_table(t, inner_carry):
-                at = pl.ds(pl.multiple_of(t * 256, 256), 256)
-                table_turned[at, :] = table[:, at].T
-                return inner_carry
-
-            lax.fori_loop(0, half_turn // 256, turn_table, 0)
 
         for quad in range(2):
             image = prior_dead[quad] * dead[p, quad]

time: 99.8 us -> 98.1 us (0.983)
  Pallas kernels: 98.5 us -> 97 us
    pallas_call x1, Pallas kernels: 95.6 us -> 94.1 us  [per_device(): pl.pallas_call(functools.partial(main_kernel, n_order, n_blk, degrees, cy...]
where the time goes in v6:
time: 98.1 us; the launch traced here: 97.7 us
  Pallas kernels  97 us (99%)
    pallas_call x1, Pallas kernels, per_device(): pl.pallas_call(functools.partial(main_kernel, n_order, n_blk, degrees, cy...  94.1 us
    pallas_call x1, Pallas kernels, per_device(): pl.pallas_call(functools.partial(unpack_kernel, degrees), in_specs=[smem]...  2.89 us

profile of v6, /device:TPU:1, one launch (start us, length us, event | category | flops | bytes accessed | tf_op | source)
XLA Modules:
  0.0 97.7 jit_solution(17683478214828415590)
XLA Ops:
  0.6 94.1 %steps.1 = (f32[2,8,3200]{2,1,0:T(8,128)}, f32[2,8,3072]{2,1,0:T(8,128)}, f32[2,8,3200]{2,1,0:T(8,128)}, f32[2,8,3072]{2,1,0:T(8,128)}) custom-call(s32[8]{0:T(128)} %orders.3, bf16[8,192,3072]{2,1,0:T(8,128)(2,1)} %leg_hbm.1, f32[2,2,8,3072]{3,2,1,0:T(8,128)} %guess_hbm.1, f32[2,2,8,3072]{3,2,1,0:T(8,128)} %rhs_hbm.1, f32[1,3072]{1,0:T(1,128)} %bitcast.5, ...), custom_call_target="tpu_custom_call" | custom-call | tf_op jit(solution)/shard_map/steps/pallas_call | solution.py:730
  94.8 2.9 %unpack.1 = (f32[2,2,8,3072]{3,2,1,0:T(8,128)}, f32[2,2,8,3072]{3,2,1,0:T(8,128)}) custom-call(s32[8]{0:T(128)} %orders.3, f32[2,8,3200]{2,1,0:T(8,128)} %get-tuple-element.6.x_live, f32[2,8,3072]{2,1,0:T(8,128)} %get-tuple-element.7.x_dead, f32[2,8,3200]{2,1,0:T(8,128)} %get-tuple-element.8.r_live, f32[2,8,3072]{2,1,0:T(8,128)} %get-tuple-element.9.r_dead), custom_call_target="tpu_custom_call" | custom-call | tf_op jit(solution)/shard_map/unpack/pallas_call | solution.py:743

commit v7 on v6

--- a/solution.py
+++ b/solution.py
@@ -651,9 +651,10 @@
         last = prior_live[quad, :, tail] * live[2, quad, :, tail] + extra_sum[quad]
         finish(quad, tail, live, r1_live, last, x_out_live, r_out_live)
     for quad in range(2):
+        finish(quad, main, live, r1_live, prior_live[quad, :, main] * live[2, quad, :, main], x_out_live, r_out_live)
+    for quad in range(2):
         wait_bytes(rs_recv0.at[2, pl.ds(0, n_blk - 1)], ag_arrive.at[2, quad])
-        last = prior_live[quad, :, main] * live[2, quad, :, main] + summed[2, quad]
-        finish(quad, main, live, r1_live, last, x_out_live, r_out_live)
+        r_out_live[quad, :, main] = r_out_live[quad, :, main] + (second * step) * summed[2, quad]
     for quad in range(2):
         wait_bytes(rs_recv0.at[2, pl.ds(0, n_blk - 1)], ag_send.at[2, quad])
 

time: 98.1 us -> 98.1 us (level)
  no operation moved by 1% of the time
where the time goes in v7:
time: 98.1 us; the launch traced here: 97.5 us
  Pallas kernels  96.8 us (99%)
    pallas_call x1, Pallas kernels, per_device(): pl.pallas_call(functools.partial(main_kernel, n_order, n_blk, degrees, cy...  94 us
    pallas_call x1, Pallas kernels, per_device(): pl.pallas_call(functools.partial(unpack_kernel, degrees), in_specs=[smem]...  2.89 us

profile of v7, /device:TPU:1, one launch (start us, length us, event | category | flops | bytes accessed | tf_op | source)
XLA Modules:
  0.0 97.5 jit_solution(15547665228211700401)
XLA Ops:
  0.6 94.0 %steps.1 = (f32[2,8,3200]{2,1,0:T(8,128)}, f32[2,8,3072]{2,1,0:T(8,128)}, f32[2,8,3200]{2,1,0:T(8,128)}, f32[2,8,3072]{2,1,0:T(8,128)}) custom-call(s32[8]{0:T(128)} %orders.3, bf16[8,192,3072]{2,1,0:T(8,128)(2,1)} %leg_hbm.1, f32[2,2,8,3072]{3,2,1,0:T(8,128)} %guess_hbm.1, f32[2,2,8,3072]{3,2,1,0:T(8,128)} %rhs_hbm.1, f32[1,3072]{1,0:T(1,128)} %bitcast.5, ...), custom_call_target="tpu_custom_call" | custom-call | tf_op jit(solution)/shard_map/steps/pallas_call | solution.py:731
  94.6 2.9 %unpack.1 = (f32[2,2,8,3072]{3,2,1,0:T(8,128)}, f32[2,2,8,3072]{3,2,1,0:T(8,128)}) custom-call(s32[8]{0:T(128)} %orders.3, f32[2,8,3200]{2,1,0:T(8,128)} %get-tuple-element.6.x_live, f32[2,8,3072]{2,1,0:T(8,128)} %get-tuple-element.7.x_dead, f32[2,8,3200]{2,1,0:T(8,128)} %get-tuple-element.8.r_live, f32[2,8,3072]{2,1,0:T(8,128)} %get-tuple-element.9.r_dead), custom_call_target="tpu_custom_call" | custom-call | tf_op jit(solution)/shard_map/unpack/pallas_call | solution.py:744
